TPU v7x, 32 devices: a whole 2x2x4 slice. The times are simulated.
32 devices in a mesh: dp: 4 (over y, core), space: 8 (over z, x).
Axes of the slice: x: 2, y: 2, z: 4, core: 2. Of those that a mesh axis runs over, the one named last changes fastest.
Arguments:
- features: bfloat16 [4, 256, 64, 512], P('dp', 'space'), may hold values from -50 to 50
- owners: int32 [4, 256, 1], P('dp', 'space'), may hold values from 0 to 7; in each aligned block of 32 rows (0 to 31, 32 to 63, ..., all dimensions but the last counted through in order) at most 8 rows name the same one
- neighbors: int32 [4, 256, 3], P('dp', 'space'), may hold values from -1 to 254, as said below
- w_reduce: bfloat16 [512, 128], replicated, may hold values from -0.25 to 0.25
- w_spatial: bfloat16 [1152, 128], replicated, may hold values from -0.1875 to 0.1875
- w_expand: bfloat16 [128, 512], replicated, may hold values from -0.5 to 0.5
- w_short: bfloat16 [512, 512], replicated, may hold values from -0.25 to 0.25
- gains_mid: float32 [2, 128], replicated, may hold values from 0.25 to 1.75
- shifts_mid: float32 [2, 128], replicated, may hold values from -2.5 to 2.5
- gains_wide: float32 [2, 512], replicated, may hold values from 0.25 to 1.75
- shifts_wide: float32 [2, 512], replicated, may hold values from -2.5 to 2.5
- cotangent: bfloat16 [4, 512, 16, 512], P('dp', 'space'), may hold values from -6 to 6
Outputs:
- block_out: bfloat16 [4, 512, 16, 512], P('dp', 'space')
- grad_features: bfloat16 [4, 256, 64, 512], P('dp', 'space')
- grad_reduce: float32 [512, 128], P('space')
- grad_spatial: float32 [1152, 128], P('space')
- grad_expand: float32 [128, 512], P('space')
- grad_short: float32 [512, 512], P('space')
- grad_gains_mid: float32 [2, 128], P(None, 'space')
- grad_shifts_mid: float32 [2, 128], P(None, 'space')
- grad_gains_wide: float32 [2, 512], P(None, 'space')
- grad_shifts_wide: float32 [2, 512], P(None, 'space')
Inputs may be any that keep to these rules, and one draw needn't show every extreme that they name: `owners`: among the 32 tiles of one block no owner is named more than 8 times. `neighbors`: entries are tile indices of the same slide or -1 for none; for tile t every index lies between t - 32 and t - 1.
All inputs are finite; a program needn't handle non-finite values.
Results may differ from a plain program's by a relative error of at most 0.02.
Values may be sent and summed in bfloat16 or wider, within the bound.
A program may use at most 64 MiB of HBM per device.

v0:
```python
import math

import jax
import jax.numpy as jnp
from jax import lax
from jax.sharding import PartitionSpec as P

GROUPS = 32
SIDE = 8


EPS = 1e-05


def passed_along(shard, axis, by):
    peers = lax.axis_size(axis)
    pairs = [(i, i + by) for i in range(peers) if 0 <= i + by < peers]
    return lax.ppermute(shard, axis, pairs)


def smooth(values):
    return values * jax.nn.sigmoid(values)


def smooth_slope(values):
    sig = jax.nn.sigmoid(values)
    return sig * (1.0 + values * (1.0 - sig))


def group_total(per_channel):
    width = per_channel.shape[-1]
    grouped = per_channel.reshape(per_channel.shape[:-1] + (GROUPS, width // GROUPS))
    return jnp.repeat(jnp.sum(grouped, axis=-1), width // GROUPS, axis=-1)


def moments(conv_out):
    values = conv_out.astype(jnp.float32)
    return jnp.stack([jnp.sum(values, axis=0), jnp.sum(values * values, axis=0)])


def grad_moments(upstream, normed):
    return jnp.stack([jnp.sum(upstream, axis=0), jnp.sum(upstream * normed, axis=0)])


def norm_forward(conv_out, totals, members, gain_row, shift_row):
    center = group_total(totals[0]) / members
    spread = group_total(totals[1]) / members - center * center
    inv_spread = lax.rsqrt(spread + EPS)
    normed = (conv_out.astype(jnp.float32) - center) * inv_spread
    return (normed, normed * gain_row + shift_row, center, inv_spread)


def norm_backward(upstream, normed, inv_spread, gain_row, totals, members):
    first = group_total(gain_row * totals[0]) / members
    second = group_total(gain_row * totals[1]) / members
    return inv_spread * (gain_row * upstream - first - normed * second)


def slide_total(partial_sums):
    return lax.psum(partial_sums, "space")


def body(
    features,
    owners,
    neighbors,
    w_reduce,
    w_spatial,
    w_expand,
    w_short,
    gains_mid,
    shifts_mid,
    gains_wide,
    shifts_wide,
    cotangent,
):
    spaces = lax.axis_size("space")
    my_index = lax.axis_index("space")
    tile_count = features.shape[1]
    positions = SIDE * SIDE
    half = SIDE // 2
    quarter = half * half
    width_in = features.shape[3]
    width_mid = w_reduce.shape[1]
    tiles_total = tile_count * spaces
    slide_count = features.shape[0] * lax.axis_size("dp")
    capacity = cotangent.shape[1] // spaces
    members_in = tiles_total * positions * (width_mid // GROUPS)
    members_mid = tiles_total * quarter * (width_mid // GROUPS)
    members_wide = tiles_total * quarter * (width_in // GROUPS)
    row_width = SIDE * width_mid
    cot_owned = cotangent[0].reshape(spaces, capacity, quarter * width_in)
    cot_home = lax.all_to_all(cot_owned, "space", split_axis=0, concat_axis=0, tiled=True)
    flat_in = features[0].reshape(tile_count * positions, width_in)
    conv_one = jnp.dot(flat_in, w_reduce, preferred_element_type=jnp.float32).astype(jnp.bfloat16)
    totals_one = slide_total(moments(conv_one))
    normed_one, pre_one, center_one, scale_one = norm_forward(
        conv_one, totals_one, members_in, gains_mid[0], shifts_mid[0]
    )
    act_one = smooth(pre_one).astype(jnp.bfloat16)
    grid_source = act_one.reshape(tile_count, SIDE, SIDE, width_mid)
    own_rims = jnp.concatenate(
        [grid_source[:, SIDE - 1], grid_source[:, :, SIDE - 1]], axis=1
    ).reshape(tile_count, 2 * row_width)
    prior_rims = passed_along(own_rims, "space", 1)
    rim_pool = jnp.concatenate([prior_rims, own_rims], axis=0)
    links = neighbors[0]
    first_index = (my_index - 1) * tile_count
    pool_slots = jnp.arange(2 * tile_count, dtype=jnp.int32)

    def pick_matrix(column):
        target = links[:, column]
        return (target[:, None] - first_index == pool_slots[None, :]) & (target[:, None] >= 0)

    match_top = pick_matrix(0)
    match_left = pick_matrix(1)
    match_corner = pick_matrix(2)
    top_row = (
        jnp.dot(
            match_top.astype(jnp.bfloat16),
            rim_pool[:, :row_width],
            preferred_element_type=jnp.float32,
        )
        .astype(jnp.bfloat16)
        .reshape(tile_count, SIDE, width_mid)
    )
    left_col = (
        jnp.dot(
            match_left.astype(jnp.bfloat16),
            rim_pool[:, row_width:],
            preferred_element_type=jnp.float32,
        )
        .astype(jnp.bfloat16)
        .reshape(tile_count, SIDE, width_mid)
    )
    corner_cell = jnp.dot(
        match_corner.astype(jnp.bfloat16),
        rim_pool[:, row_width - width_mid : row_width],
        preferred_element_type=jnp.float32,
    ).astype(jnp.bfloat16)
    grid_act = act_one.reshape(tile_count, SIDE, SIDE, width_mid)
    first_line = jnp.concatenate([corner_cell[:, None], top_row], axis=1)
    lower_rows = jnp.concatenate([left_col[:, :, None], grid_act], axis=2)
    padded = jnp.concatenate([first_line[:, None], lower_rows], axis=1)
    columns = jnp.concatenate(
        [
            padded[
                :, offset_row : offset_row + SIDE - 1 : 2, offset_col : offset_col + SIDE - 1 : 2
            ]
            for offset_row in range(3)
            for offset_col in range(3)
        ],
        axis=-1,
    ).reshape(tile_count * quarter, 9 * width_mid)
    conv_two = jnp.dot(columns, w_spatial, preferred_element_type=jnp.float32).astype(jnp.bfloat16)
    totals_two = slide_total(moments(conv_two))
    normed_two, pre_two, center_two, scale_two = norm_forward(
        conv_two, totals_two, members_mid, gains_mid[1], shifts_mid[1]
    )
    act_two = smooth(pre_two).astype(jnp.bfloat16)
    conv_three = jnp.dot(act_two, w_expand, preferred_element_type=jnp.float32).astype(jnp.bfloat16)
    sub_in = (
        features[0]
        .reshape(tile_count, SIDE, SIDE, width_in)[:, ::2, ::2]
        .reshape(tile_count * quarter, width_in)
    )
    conv_short = jnp.dot(sub_in, w_short, preferred_element_type=jnp.float32).astype(jnp.bfloat16)
    totals_wide = slide_total(jnp.concatenate([moments(conv_three), moments(conv_short)], axis=0))
    normed_three, pre_three, center_three, scale_three = norm_forward(
        conv_three, totals_wide[:2], members_wide, gains_wide[0], shifts_wide[0]
    )
    normed_short, pre_short, center_short, scale_short = norm_forward(
        conv_short, totals_wide[2:], members_wide, gains_wide[1], shifts_wide[1]
    )
    summed = pre_three + pre_short
    result = smooth(summed).astype(jnp.bfloat16)
    owner_of = owners[0][:, 0]
    owner_hits = (owner_of[:, None] == jnp.arange(spaces, dtype=jnp.int32)[None, :]).astype(
        jnp.int32
    )
    before = jnp.cumsum(owner_hits, axis=0) - owner_hits
    rank_in = jnp.sum(before * owner_hits, axis=1)
    slot_of = owner_of * capacity + rank_in
    dispatch = (jnp.arange(spaces * capacity, dtype=jnp.int32)[:, None] == slot_of[None, :]).astype(
        jnp.bfloat16
    )
    outgoing = (
        jnp.dot(
            dispatch,
            result.reshape(tile_count, quarter * width_in),
            preferred_element_type=jnp.float32,
        )
        .astype(jnp.bfloat16)
        .reshape(spaces, capacity, quarter * width_in)
    )
    arrived = lax.all_to_all(outgoing, "space", split_axis=0, concat_axis=0, tiled=True)
    block_out = arrived.reshape(1, spaces * capacity, quarter, width_in)
    picked = jnp.dot(
        dispatch.T,
        cot_home.reshape(spaces * capacity, quarter * width_in),
        preferred_element_type=jnp.float32,
    ).reshape(tile_count * quarter, width_in)
    upstream = picked * smooth_slope(summed)
    totals_back = slide_total(
        jnp.concatenate(
            [grad_moments(upstream, normed_three), grad_moments(upstream, normed_short)], axis=0
        )
    )
    dconv_three = norm_backward(
        upstream, normed_three, scale_three, gains_wide[0], totals_back[:2], members_wide
    ).astype(jnp.bfloat16)
    dconv_short = norm_backward(
        upstream, normed_short, scale_short, gains_wide[1], totals_back[2:], members_wide
    ).astype(jnp.bfloat16)
    grad_expand_part = jnp.dot(act_two.T, dconv_three, preferred_element_type=jnp.float32)
    grad_short_part = jnp.dot(sub_in.T, dconv_short, preferred_element_type=jnp.float32)
    back_two = jnp.dot(dconv_three, w_expand.T, preferred_element_type=jnp.float32)
    back_two = back_two * smooth_slope(pre_two)
    totals_two_back = slide_total(grad_moments(back_two, normed_two))
    dconv_two = norm_backward(
        back_two, normed_two, scale_two, gains_mid[1], totals_two_back, members_mid
    ).astype(jnp.bfloat16)
    grad_spatial_part = jnp.dot(columns.T, dconv_two, preferred_element_type=jnp.float32)
    back_cols = jnp.dot(dconv_two, w_spatial.T, preferred_element_type=jnp.float32).reshape(
        tile_count, half, half, 9, width_mid
    )
    back_pad = jnp.zeros((tile_count, SIDE + 1, SIDE + 1, width_mid), jnp.float32)
    for offset_row in range(3):
        for offset_col in range(3):
            back_pad = back_pad.at[
                :, offset_row : offset_row + SIDE - 1 : 2, offset_col : offset_col + SIDE - 1 : 2
            ].add(back_cols[:, :, :, 3 * offset_row + offset_col])
    to_top = back_pad[:, 0, 1:].reshape(tile_count, row_width)
    to_left = back_pad[:, 1:, 0].reshape(tile_count, row_width)
    to_corner = back_pad[:, 0, 0]
    rows_back = jnp.dot(match_top.astype(jnp.float32).T, to_top, precision=lax.Precision.HIGHEST)
    corner_back = jnp.dot(
        match_corner.astype(jnp.float32).T, to_corner, precision=lax.Precision.HIGHEST
    )
    rows_back = rows_back.at[:, row_width - width_mid :].add(corner_back)
    cols_back = jnp.dot(match_left.astype(jnp.float32).T, to_left, precision=lax.Precision.HIGHEST)
    rim_back = jnp.concatenate([rows_back, cols_back], axis=1)
    from_next = passed_along(rim_back[:tile_count].astype(jnp.bfloat16), "space", -1).astype(
        jnp.float32
    )
    own_back = (rim_back[tile_count:] + from_next).reshape(tile_count, 2 * SIDE, width_mid)
    inner = back_pad[:, 1:, 1:]
    inner = inner.at[:, SIDE - 1].add(own_back[:, :SIDE]).at[:, :, SIDE - 1].add(own_back[:, SIDE:])
    back_one = (inner * smooth_slope(pre_one).reshape(tile_count, SIDE, SIDE, width_mid)).reshape(
        tile_count * positions, width_mid
    )
    totals_one_back = slide_total(grad_moments(back_one, normed_one))
    dconv_one = norm_backward(
        back_one, normed_one, scale_one, gains_mid[0], totals_one_back, members_in
    ).astype(jnp.bfloat16)
    grad_reduce_part = jnp.dot(flat_in.T, dconv_one, preferred_element_type=jnp.float32)
    back_in = jnp.dot(dconv_one, w_reduce.T, preferred_element_type=jnp.float32).reshape(
        tile_count, SIDE, SIDE, width_in
    )
    back_short = jnp.dot(dconv_short, w_short.T, preferred_element_type=jnp.float32).reshape(
        tile_count, half, half, width_in
    )
    back_in = back_in.at[:, ::2, ::2].add(back_short)
    grad_features = back_in.reshape(1, tile_count, positions, width_in).astype(jnp.bfloat16)
    gain_mid_full = jnp.stack([totals_one_back[1], totals_two_back[1]])
    shift_mid_full = jnp.stack([totals_one_back[0], totals_two_back[0]])
    gain_wide_full = jnp.stack([totals_back[1], totals_back[3]])
    shift_wide_full = jnp.stack([totals_back[0], totals_back[2]])

    def own_part(array):
        share = array.shape[1] // spaces
        return lax.dynamic_slice_in_dim(array, my_index * share, share, 1)

    share_reduce, share_spatial, share_expand, share_short = (
        lax.psum_scatter(
            grad_reduce_part.astype(jnp.bfloat16), "space", scatter_dimension=0, tiled=True
        ).astype(jnp.float32),
        lax.psum_scatter(
            grad_spatial_part.astype(jnp.bfloat16), "space", scatter_dimension=0, tiled=True
        ).astype(jnp.float32),
        lax.psum_scatter(
            grad_expand_part.astype(jnp.bfloat16), "space", scatter_dimension=0, tiled=True
        ).astype(jnp.float32),
        lax.psum_scatter(
            grad_short_part.astype(jnp.bfloat16), "space", scatter_dimension=0, tiled=True
        ).astype(jnp.float32),
    )
    summed_all = (
        lax.psum(share_reduce.astype(jnp.bfloat16), "dp").astype(jnp.float32),
        lax.psum(share_spatial.astype(jnp.bfloat16), "dp").astype(jnp.float32),
        lax.psum(share_expand.astype(jnp.bfloat16), "dp").astype(jnp.float32),
        lax.psum(share_short.astype(jnp.bfloat16), "dp").astype(jnp.float32),
        lax.psum(own_part(gain_mid_full).astype(jnp.bfloat16), "dp").astype(jnp.float32),
        lax.psum(own_part(shift_mid_full).astype(jnp.bfloat16), "dp").astype(jnp.float32),
        lax.psum(own_part(gain_wide_full).astype(jnp.bfloat16), "dp").astype(jnp.float32),
        lax.psum(own_part(shift_wide_full).astype(jnp.bfloat16), "dp").astype(jnp.float32),
    )
    scale_in = 1.0 / math.sqrt(slide_count * tiles_total * positions)
    scale_out = 1.0 / math.sqrt(slide_count * tiles_total * quarter)
    mid_scale = jnp.array([[scale_in], [scale_out]], jnp.float32)
    return (
        block_out,
        grad_features,
        summed_all[0] * scale_in,
        summed_all[1] * scale_out,
        summed_all[2] * scale_out,
        summed_all[3] * scale_out,
        summed_all[4] * mid_scale,
        summed_all[5] * mid_scale,
        summed_all[6] * scale_out,
        summed_all[7] * scale_out,
    )


def solution(mesh):
    placed = (
        P("dp", "space", None, None),
        P("dp", "space", None),
        P("dp", "space", None),
        P(),
        P(),
        P(),
        P(),
        P(),
        P(),
        P(),
        P(),
        P("dp", "space", None, None),
    )
    return jax.shard_map(
        body,
        mesh=mesh,
        in_specs=placed,
        out_specs=(
            P("dp", "space", None, None),
            P("dp", "space", None, None),
            P("space", None),
            P("space", None),
            P("space", None),
            P("space", None),
            P(None, "space"),
            P(None, "space"),
            P(None, "space"),
            P(None, "space"),
        ),
        check_vma=False,
    )
```

profile of v0, /device:TPU:0, one launch (start us, length us, event | category | flops | bytes accessed | tf_op | source)
XLA Modules:
  0.0 866.7 jit_solution(16874853562494326843)
XLA Ops:
  7.2 2.4 reshape_squeeze.49
  9.6 7.4 all-to-all-start.1
  17.1 2.3 fusion.91
  19.4 29.6 %psum.98 = f32[2,128]{1,0:T(2,128)S(1)} all-reduce(f32[2,128]{1,0:T(2,128)S(1)} %pad_maximum_fusion.5), channel_id=1, replica_groups=mesh['dp'=4,'space'=8] {'space'}, use_global_device_ids=true, to_apply=%region_4.0 | all-reduce | flops 256 | bytes 2048 | tf_op jit(solution)/shard_map/psum | solution.py:60
  50.4 1.5 add_multiply_fusion
  52.9 3.8 collective-permute-start
  56.7 5.0 slice.296
  61.7 37.5 %slice.295 = bf16[32,4,4,128]{3,2,1,0:T(4,128)(2,1)} slice(bf16[32,8,8,128]{3,2,1,0:T(8,128)(2,1)S(1)} %bitcast.223), slice={[0:32:1], [1:8:2], [0:7:2], [0:128:1]} | slice | bytes 262144 | tf_op jit(solution)/shard_map/slice | solution.py:147
  99.3 37.3 %slice.293 = bf16[32,4,4,128]{3,2,1,0:T(4,128)(2,1)} slice(bf16[32,8,8,128]{3,2,1,0:T(8,128)(2,1)S(1)} %bitcast.224), slice={[0:32:1], [0:7:2], [1:8:2], [0:128:1]} | slice | bytes 262144 | tf_op jit(solution)/shard_map/slice | solution.py:147
  136.6 37.3 %slice.292 = bf16[32,4,4,128]{3,2,1,0:T(4,128)(2,1)} slice(bf16[32,8,8,128]{3,2,1,0:T(8,128)(2,1)S(1)} %bitcast.225), slice={[0:32:1], [0:7:2], [0:7:2], [0:128:1]} | slice | bytes 262144 | tf_op jit(solution)/shard_map/slice | solution.py:147
  183.0 47.3 %slice.301 = bf16[32,4,4,512]{3,2,1,0:T(4,128)(2,1)S(1)} slice(bf16[32,8,8,512]{3,2,1,0:T(8,128)(2,1)} %bitcast.218), slice={[0:32:1], [0:8:2], [0:8:2], [0:512:1]} | slice | bytes 1048576 | tf_op jit(solution)/shard_map/slice | solution.py:163
  230.5 1.8 convert_reduce_fusion
  234.2 37.4 %slice.290 = bf16[32,4,4,128]{3,2,1,0:T(4,128)(2,1)} slice(bf16[32,9,9,128]{3,2,1,0:T(8,128)(2,1)S(1)} %maximum_maximum_fusion), slice={[0:32:1], [0:7:2], [2:9:2], [0:128:1]} | slice | bytes 262144 | tf_op jit(solution)/shard_map/slice | solution.py:147
  271.6 37.3 %slice.289 = bf16[32,4,4,128]{3,2,1,0:T(4,128)(2,1)} slice(bf16[32,9,9,128]{3,2,1,0:T(8,128)(2,1)S(1)} %maximum_maximum_fusion), slice={[0:32:1], [0:7:2], [1:8:2], [0:128:1]} | slice | bytes 262144 | tf_op jit(solution)/shard_map/slice | solution.py:147
  308.9 36.9 %slice.288 = bf16[32,4,4,128]{3,2,1,0:T(4,128)(2,1)} slice(bf16[32,9,9,128]{3,2,1,0:T(8,128)(2,1)S(1)} %maximum_maximum_fusion), slice={[0:32:1], [0:7:2], [0:7:2], [0:128:1]} | slice | bytes 262144 | tf_op jit(solution)/shard_map/slice | solution.py:147
  346.2 2.9 slice.291
  349.1 4.7 slice.294
  353.9 1.6 constant_dynamic-update-slice_fusion.10
  355.5 1.6 constant_dynamic-update-slice_fusion.9
  357.1 1.6 constant_dynamic-update-slice_fusion.8
  362.9 2.4 reshape.378
  365.9 20.4 %psum.99 = f32[2,128]{1,0:T(2,128)S(1)} all-reduce(f32[2,128]{1,0:T(2,128)S(1)} %pad_maximum_fusion.6), channel_id=1, replica_groups=mesh['dp'=4,'space'=8] {'space'}, use_global_device_ids=true, to_apply=%region_9.0 | all-reduce | flops 256 | bytes 2048 | tf_op jit(solution)/shard_map/psum | solution.py:60
  387.2 2.0 convert_reduce_fusion.1
  389.3 17.4 %psum.100 = f32[4,512]{1,0:T(4,128)S(1)} all-reduce(f32[4,512]{1,0:T(4,128)S(1)} %pad_maximum_fusion.3), channel_id=1, replica_groups=mesh['dp'=4,'space'=8] {'space'}, use_global_device_ids=true, to_apply=%region_16.0 | all-reduce | flops 2048 | bytes 16384 | tf_op jit(solution)/shard_map/psum | solution.py:60
  408.2 1.6 fusion.34
  411.0 3.1 fusion.15
  414.1 19.4 %psum.101 = f32[4,512]{1,0:T(4,128)S(1)} all-reduce(f32[4,512]{1,0:T(4,128)S(1)} %pad_maximum_fusion.4), channel_id=1, replica_groups=mesh['dp'=4,'space'=8] {'space'}, use_global_device_ids=true, to_apply=%region_24.25 | all-reduce | flops 2048 | bytes 16384 | tf_op jit(solution)/shard_map/psum | solution.py:60
  435.6 1.8 fusion.28
  439.3 1.4 fusion.92
  440.7 17.3 %psum.102 = f32[2,128]{1,0:T(2,128)S(1)} all-reduce(f32[2,128]{1,0:T(2,128)S(1)} %pad_maximum_fusion.7), channel_id=1, replica_groups=mesh['dp'=4,'space'=8] {'space'}, use_global_device_ids=true, to_apply=%region_29.30 | all-reduce | flops 256 | bytes 2048 | tf_op jit(solution)/shard_map/psum | solution.py:60
  460.2 1.9 fusion.102
  462.1 4.2 reshape.385
  466.3 9.8 %fusion.95 = (f32[32,4,4,1,128]{4,3,2,1,0:T(1,128)S(1)}, f32[32,4,4,1,128]{4,3,2,1,0:T(1,128)S(1)}, f32[32,4,4,1,128]{4,3,2,1,0:T(1,128)S(1)}, f32[32,4,4,1,128]...) fusion(f32[32,4,4,9,128]{4,3,2,1,0:T(8,128)} %reshape.385), kind=kLoop, calls=%fused_computation.259 | loop fusion | bytes 4718592 | tf_op jit(solution)/shard_map/slice | solution.py:232
  483.4 2.2 scatter_fusion
  485.6 2.2 scatter_fusion.1
  487.8 2.2 scatter_fusion.2
  490.0 2.2 scatter_fusion.3
  492.1 2.2 scatter_fusion.4
  494.3 2.2 scatter_fusion.5
  496.5 2.2 scatter_fusion.6
  498.7 2.2 scatter_fusion.7
  500.8 2.2 scatter_fusion.8
  503.1 1.5 fusion.104
  506.6 1.5 collective-permute-start.1
  509.8 2.1 reshape.380
  511.9 1.3 fusion.79
  516.5 20.0 %psum.103 = f32[2,128]{1,0:T(2,128)S(1)} all-reduce(f32[2,128]{1,0:T(2,128)S(1)} %pad_maximum_fusion.8), channel_id=1, replica_groups=mesh['dp'=4,'space'=8] {'space'}, use_global_device_ids=true, to_apply=%region_43.44 | all-reduce | flops 256 | bytes 2048 | tf_op jit(solution)/shard_map/psum | solution.py:60
  543.6 55.0 %reduce-scatter.13.cloned.1.call-done = bf16[64,128]{1,0:T(8,128)(2,1)} async-done(((bf16[512,128]{1,0:T(8,128)(2,1)}), bf16[64,128]{1,0:T(8,128)(2,1)}) %reduce-scatter.13.cloned.1.call-update) | async-done | bytes 16400
  598.6 1.4 copy.93
  600.0 61.8 %reduce-scatter.11.cloned.1.call-done = bf16[16,512]{1,0:T(8,128)(2,1)} async-done(((bf16[128,512]{1,0:T(8,128)(2,1)}), bf16[16,512]{1,0:T(8,128)(2,1)}) %reduce-scatter.11.cloned.1.call-update) | async-done | bytes 16400 | tf_op jit(solution)/shard_map/reduce_scatter | solution.py:281
  661.8 61.7 %reduce-scatter.9.cloned.1.call-done = bf16[144,128]{1,0:T(8,128)(2,1)} async-done(((bf16[1152,128]{1,0:T(8,128)(2,1)}), bf16[144,128]{1,0:T(8,128)(2,1)}) %reduce-scatter.9.cloned.1.call-update) | async-done | bytes 36880 | tf_op jit(solution)/shard_map/reduce_scatter | solution.py:278
  723.5 1.4 fusion
  726.9 3.7 all-to-all-start
  732.2 4.3 copy.88
  736.5 3.5 scatter_fusion.9
  740.0 2.5 convert_element_type.172
  742.6 2.5 copy.89
  745.1 12.2 %all-reduce.6.cloned.1.call-done = (bf16[64,128]{0,1:T(8,128)(2,1)}, bf16[144,128]{1,0:T(8,128)(2,1)}, bf16[16,512]{1,0:T(8,128)(2,1)}, bf16[2,16]{1,0:T(2,128)(...) async-done(((bf16[64,128]{0,1:T(8,128)(2,1)}, bf16[144,128]{1,0:T(8,128)(2,1)}, bf16[16,512]{1,0:T(8,128)(2,1)}, bf16[2,16]{1,0:T(2,128)(2,1)}, ...) | async-done | bytes 70288 | tf_op jit(solution)/shard_map/psum | solution.py:289
  759.7 1.3 convert_multiply_fusion.5
  761.8 1.4 convert_multiply_fusion.3
  763.2 60.4 %reduce-scatter.15.cloned.1.call-done = bf16[64,512]{1,0:T(8,128)(2,1)} async-done(((bf16[512,512]{1,0:T(8,128)(2,1)}), bf16[64,512]{1,0:T(8,128)(2,1)}) %reduce-scatter.15.cloned.1.call-update) | async-done | bytes 65552
  823.6 1.6 copy.95
  827.2 29.6 %all-reduce.4.cloned.1.call-done = bf16[64,512]{0,1:T(8,128)(2,1)} async-done(((bf16[64,512]{0,1:T(8,128)(2,1)}), bf16[64,512]{0,1:T(8,128)(2,1)}) %all-reduce.4.cloned.1.call-update) | async-done | bytes 65552 | tf_op jit(solution)/shard_map/psum | solution.py:292
  858.5 1.3 copy.103
  (354 shorter events, 59.4 us)
Async XLA Ops:
  7.2 223.2 %copy-start = (bf16[512,512]{1,0:T(8,128)(2,1)S(1)}, bf16[512,512]{1,0:T(8,128)(2,1)}, u32[]{:S(2)}) copy-start(bf16[512,512]{1,0:T(8,128)(2,1)} %param.25) | copy-start | bytes 1572868
  9.6 7.4 copy-start.15
  9.6 398.6 %all-to-all-start.1 = ((bf16[8,8,8192]{2,1,0:T(8,128)(2,1)}), bf16[8,8,8192]{2,1,0:T(8,128)(2,1)}, u32[]{:S(2)}, u32[]{:S(2)}) async-start(bf16[8,8,8192]{2,1,0:T(8,128)(2,1)} %reshape_squeeze.49), calls=%async_computation.1 | async-start | bytes 2097152 | tf_op jit(solution)/shard_map/all_to_all | solution.py:93
  17.0 581.6 %reduce-scatter.13.cloned.1.call-start = ((), (), s32[]{:S(2)}) async-start(), calls=%async_computation.9 | async-start | bytes 147456
  17.0 32.8 %copy-start.43 = (f32[2,128]{1,0:T(2,128)S(1)}, f32[2,128]{1,0:T(2,128)}, u32[]{:S(2)}) copy-start(f32[2,128]{1,0:T(2,128)} %param.26) | copy-start | bytes 3076
  17.1 32.8 %copy-start.56 = (f32[2,128]{1,0:T(2,128)S(1)}, f32[2,128]{1,0:T(2,128)}, u32[]{:S(2)}) copy-start(f32[2,128]{1,0:T(2,128)} %param.27) | copy-start | bytes 3076
  49.5 2.4 copy-start.25
  51.9 122.8 %copy-start.55 = (s32[1,32,3]{1,0,2:T(1,128)S(1)}, s32[1,32,3]{1,0,2:T(1,128)}, u32[]{:S(2)}) copy-start(s32[1,32,3]{1,0,2:T(1,128)} %param.21) | copy-start | bytes 1156
  51.9 123.9 %copy-start.42 = (f32[2,512]{1,0:T(2,128)S(1)}, f32[2,512]{1,0:T(2,128)}, u32[]{:S(2)}) copy-start(f32[2,512]{1,0:T(2,128)} %param.29) | copy-start | bytes 12292
  51.9 124.5 %copy-start.24 = (f32[2,512]{1,0:T(2,128)S(1)}, f32[2,512]{1,0:T(2,128)}, u32[]{:S(2)}) copy-start(f32[2,512]{1,0:T(2,128)} %param.28) | copy-start | bytes 12292
  51.9 130.2 %copy-start.48 = (s32[1,32,1]{1,2,0:T(1,128)S(1)}, s32[1,32,1]{1,2,0:T(1,128)}, u32[]{:S(2)}) copy-start(s32[1,32,1]{1,2,0:T(1,128)} %param.20) | copy-start | bytes 388
  52.9 180.0 %collective-permute-start = (bf16[32,2048]{1,0:T(8,128)(2,1)}, bf16[32,2048]{1,0:T(8,128)(2,1)S(1)}, u32[]{:S(2)}, u32[]{:S(2)}) collective-permute-start(bf16[32,2048]{1,0:T(8,128)(2,1)} %bitcast.213), channel_id=1, source_target_pairs={{0,1},{1,2},{2,3},{3,4},{4,5},{5,6},{6,7},{8,9},{9,10},{10,11},{11... | collective-permute-start | bytes 393224 | tf_op jit(solution)/shard_map/ppermute | solution.py:18
  230.4 2.5 copy-start.17
  230.4 1.9 copy-start.49
  230.4 1.9 copy-start.60
  230.4 2.5 copy-start.58
  230.4 2.5 copy-start.61
  230.5 2.7 copy-start.32
  230.5 2.7 copy-start.36
  230.5 2.9 copy-start.34
  230.5 2.9 copy-start.38
  346.2 13.2 %copy-start.21 = (bf16[32,4,4,128]{3,2,1,0:T(4,128)(2,1)S(1)}, bf16[32,4,4,128]{3,2,1,0:T(4,128)(2,1)}, u32[]{:S(2)}) copy-start(bf16[32,4,4,128]{3,2,1,0:T(4,128)(2,1)} %slice.292) | copy-start | bytes 393220
  346.2 13.9 %copy-start.20 = (bf16[32,4,4,128]{3,2,1,0:T(4,128)(2,1)S(1)}, bf16[32,4,4,128]{3,2,1,0:T(4,128)(2,1)}, u32[]{:S(2)}) copy-start(bf16[32,4,4,128]{3,2,1,0:T(4,128)(2,1)} %slice.293) | copy-start | bytes 393220
  346.2 15.2 %copy-start.19 = (bf16[32,4,4,128]{3,2,1,0:T(4,128)(2,1)S(1)}, bf16[32,4,4,128]{3,2,1,0:T(4,128)(2,1)}, u32[]{:S(2)}) copy-start(bf16[32,4,4,128]{3,2,1,0:T(4,128)(2,1)} %slice.295) | copy-start | bytes 393220
  362.2 3.1 copy-start.11
  365.3 24.0 %copy-start.2 = (bf16[512,1152]{1,0:T(8,128)(2,1)}, bf16[512,1152]{1,0:T(8,128)(2,1)S(1)}, u32[]{:S(2)}) copy-start(bf16[512,1152]{1,0:T(8,128)(2,1)S(1)} %reshape.378) | copy-start | bytes 3538948
  365.3 21.9 %copy-start.53 = (f32[128]{0:T(128)S(1)}, f32[128]{0:T(128)}, u32[]{:S(2)}) copy-start(f32[128]{0:T(128)} %get-tuple-element.170) | copy-start | bytes 1540
  365.3 21.9 %copy-start.65 = (f32[128]{0:T(128)S(1)}, f32[128]{0:T(128)}, u32[]{:S(2)}) copy-start(f32[128]{0:T(128)} %get-tuple-element.160) | copy-start | bytes 1540
  365.8 41.4 %copy-start.13 = (f32[512,128]{1,0:T(8,128)}, f32[512,128]{1,0:T(8,128)S(1)}, u32[]{:S(2)}) copy-start(f32[512,128]{1,0:T(8,128)S(1)} %get-tuple-element.165) | copy-start | bytes 786436
  365.8 23.4 %copy-start.50 = (f32[512]{0:T(512)S(1)}, f32[512]{0:T(512)}, u32[]{:S(2)}) copy-start(f32[512]{0:T(512)} %get-tuple-element.83) | copy-start | bytes 6148
  365.8 23.4 %copy-start.51 = (f32[512]{0:T(512)S(1)}, f32[512]{0:T(512)}, u32[]{:S(2)}) copy-start(f32[512]{0:T(512)} %get-tuple-element.84) | copy-start | bytes 6148
  386.7 52.5 %copy-start.52 = (f32[128]{0:T(128)}, f32[128]{0:T(128)S(1)}, u32[]{:S(2)}) copy-start(f32[128]{0:T(128)S(1)} %div.98) | copy-start | bytes 1540
  387.2 52.1 %copy-start.66 = (f32[128]{0:T(128)}, f32[128]{0:T(128)S(1)}, u32[]{:S(2)}) copy-start(f32[128]{0:T(128)S(1)} %add_rsqrt_fusion.2) | copy-start | bytes 1540
  387.2 21.0 %copy-start.46 = (s32[32]{0:T(128)S(1)}, s32[32]{0:T(128)}, u32[]{:S(2)}) copy-start(s32[32]{0:T(128)} %multiply_add_fusion.2) | copy-start | bytes 388
  435.6 2.6 copy-start.14
  437.5 65.6 %copy-start.8 = (bf16[512,512]{1,0:T(8,128)(2,1)}, bf16[512,512]{1,0:T(8,128)(2,1)S(1)}, u32[]{:S(2)}) copy-start(bf16[512,512]{1,0:T(8,128)(2,1)S(1)} %get-tuple-element.127) | copy-start | bytes 1572868
  437.5 1.7 copy-start.67
  439.2 18.8 %copy-start.44 = (f32[2,128]{1,0:T(2,128)S(1)}, f32[2,128]{1,0:T(2,128)}, u32[]{:S(2)}) copy-start(f32[2,128]{1,0:T(2,128)} %param.26) | copy-start | bytes 3076
  439.2 20.2 %copy-start.54 = (f32[128]{0:T(128)S(1)}, f32[128]{0:T(128)}, u32[]{:S(2)}) copy-start(f32[128]{0:T(128)} %get-tuple-element.170) | copy-start | bytes 1540
  439.3 20.9 %copy-start.12 = (bf16[1152,128]{1,0:T(8,128)(2,1)S(1)}, bf16[1152,128]{1,0:T(8,128)(2,1)}, u32[]{:S(2)}) copy-start(bf16[1152,128]{1,0:T(8,128)(2,1)} %param.23) | copy-start | bytes 884740
  503.1 2.1 copy-start.33
  503.1 2.1 copy-start.37
  503.1 2.5 copy-start.59
  503.1 2.5 copy-start.62
  504.6 3.5 copy-start.28
  504.6 3.5 copy-start.29
  506.6 7.2 collective-permute-start.1
  511.9 2.9 copy-start.4
  516.2 20.3 %copy-start.45 = (f32[2,128]{1,0:T(2,128)S(1)}, f32[2,128]{1,0:T(2,128)}, u32[]{:S(2)}) copy-start(f32[2,128]{1,0:T(2,128)} %param.26) | copy-start | bytes 3076
  516.2 21.2 %copy-start.41 = (f32[128]{0:T(128)S(1)}, f32[128]{0:T(128)}, u32[]{:S(2)}) copy-start(f32[128]{0:T(128)} %copy-done.40) | copy-start | bytes 1540
  539.4 2.2 copy-start.9
  539.5 2.2 copy-start.18
  540.2 121.6 %reduce-scatter.11.cloned.1.call-start = ((), (), s32[]{:S(2)}) async-start(), calls=%async_computation.7 | async-start | bytes 147456 | tf_op jit(solution)/shard_map/reduce_scatter | solution.py:281
  541.5 182.0 %copy-start.7 = (bf16[32,8192]{1,0:T(8,128)(2,1)S(1)}, bf16[32,8192]{1,0:T(8,128)(2,1)}, u32[]{:S(2)}) copy-start(bf16[32,8192]{1,0:T(8,128)(2,1)} %reshape.380) | copy-start | bytes 1572868
  541.5 182.0 %copy-start.47 = (s32[32]{0:T(128)S(1)}, s32[32]{0:T(128)}, u32[]{:S(2)}) copy-start(s32[32]{0:T(128)} %multiply_add_fusion.2) | copy-start | bytes 388
  541.6 181.9 %reduce-scatter.9.cloned.1.call-start = ((), (), s32[]{:S(2)}) async-start(), calls=%async_computation.6 | async-start | bytes 331776 | tf_op jit(solution)/shard_map/reduce_scatter | solution.py:278
  542.3 214.9 %all-reduce.6.cloned.1.call-start = ((), (), s32[]{:S(2)}) async-start(), calls=%async_computation.11 | async-start | bytes 176128 | tf_op jit(solution)/shard_map/psum | solution.py:289
  723.5 2.4 copy-start.6
  726.9 4.6 copy-start.16
  726.9 131.6 %all-to-all-start = ((bf16[8,8,8192]{2,1,0:T(8,128)(2,1)}), bf16[8,8,8192]{2,1,0:T(8,128)(2,1)S(1)}, u32[]{:S(2)}, u32[]{:S(2)}) async-start(bf16[8,8,8192]{2,1,0:T(8,128)(2,1)} %fusion), calls=%async_computation | async-start | bytes 2097152 | tf_op jit(solution)/shard_map/all_to_all | solution.py:196
  730.6 93.1 %reduce-scatter.15.cloned.1.call-start = ((), (), s32[]{:S(2)}) async-start(), calls=%async_computation.10 | async-start | bytes 589824
  731.2 125.6 %all-reduce.4.cloned.1.call-start = ((), (), s32[]{:S(2)}) async-start(), calls=%async_computation.8 | async-start | bytes 262144 | tf_op jit(solution)/shard_map/psum | solution.py:292
  732.2 4.3 copy-start.23
  742.6 15.9 %copy-start.57 = (f32[2]{0:T(128)S(1)}, f32[2]{0:T(128)}, u32[]{:S(2)}) copy-start(f32[2]{0:T(128)} %constant.158) | copy-start | bytes 28
  (14 other events, 17.7 us)
Sparse Core Ops, SparseCore 0:
  540.4 58.1 reduce-scatter.12
  601.9 59.8 reduce-scatter.10
  665.7 57.7 reduce-scatter.8
  727.3 29.8 all-reduce.5
  760.8 62.8 reduce-scatter.14
  826.4 30.3 all-reduce.3
where the time goes:
time: 872 us; the launch traced here: 867 us
  local copies, waits for them, and re-layouts  357 us (41%)
  waiting for transfers between devices  282 us (32%)
  blocking collectives  124 us (14%)
  other arithmetic  51.4 us (6%)
  matrix products  19.8 us (2%)
  starting transfers between devices  16.9 us (2%)
  between operations  15.7 us (2%)
    slice x9, local copies, waits for them, and re-layouts, body(): padded[:, offset_row:offset_row + SIDE - 1:2, offset_col:offset_col + SID...  236 us
    psum x6, blocking collectives, slide_total(): return lax.psum(partial_sums, 'space')  124 us
    unnamed x8, waiting for transfers between devices  116 us
    reduce_scatter x1, waiting for transfers between devices, body(): lax.psum_scatter(grad_expand_part.astype(jnp.bfloat16), 'space', scatter_...  61.8 us
    reduce_scatter x1, waiting for transfers between devices, body(): lax.psum_scatter(grad_spatial_part.astype(jnp.bfloat16), 'space', scatter...  61.7 us
    slice x1, local copies, waits for them, and re-layouts, body(): features[0].reshape(tile_count, SIDE, SIDE, width_in)[:, ::2, ::2]  47.3 us
    psum x1, waiting for transfers between devices, body(): lax.psum(share_short.astype(jnp.bfloat16), 'dp').astype(jnp.float32)  29.6 us
    unnamed x158, local copies, waits for them, and re-layouts  21.5 us
  transfers between devices with their start and end apart: 10, of which 7 were waited for; matrix products, arithmetic and copies ran while one was open for 41% of the time, Pallas kernels for 0%

commit v1 on v0

v1 whole, which is shorter than its diff:
```python
import functools
import math

import jax
import jax.numpy as jnp
import numpy as np
from jax import lax
from jax.experimental import pallas as pl
from jax.experimental.pallas import tpu as pltpu
from jax.sharding import PartitionSpec as P

GROUPS = 32
SIDE = 8
HALF = SIDE // 2
Q = HALF * HALF
EPS = 1e-05
MESH = pl.DeviceIdType.MESH
F32 = jnp.float32
BF16 = jnp.bfloat16
STEP = 4
BLOCK = 128


def sigmoid(v):
    return 1.0 / (1.0 + jnp.exp(-v))


def smooth(v):
    return v * sigmoid(v)


def slope(v):
    s = sigmoid(v)
    return s * (1.0 + v * (1.0 - s))


def mm(a, b):
    return lax.dot_general(a, b, (((1,), (0,)), ((), ())), preferred_element_type=F32)


def mm_t(a, b):
    return lax.dot_general(a, b, (((1,), (1,)), ((), ())), preferred_element_type=F32)


def t_mm(a, b):
    return lax.dot_general(a, b, (((0,), (0,)), ((), ())), preferred_element_type=F32)


def group_sum(rows):
    width = rows.shape[-1]
    each = width // GROUPS
    a = lax.broadcasted_iota(jnp.int32, (width, width), 0) // each
    b = lax.broadcasted_iota(jnp.int32, (width, width), 1) // each
    same = jnp.where(a == b, 1.0, 0.0).astype(F32)
    return lax.dot_general(
        rows,
        same,
        (((1,), (0,)), ((), ())),
        precision=lax.Precision.HIGHEST,
        preferred_element_type=F32,
    )


def norm_of(tot, first, width, members):
    g = group_sum(tot[:, :width])
    center = g[first : first + 1] / members
    spread = g[first + 1 : first + 2] / members - center * center
    return center, lax.rsqrt(spread + EPS)


def back_of(tot, first, second, gain, width, members):
    g = group_sum(tot[:, :width] * gain)
    return g[first : first + 1] / members, g[second : second + 1] / members


def sums(v):
    return jnp.sum(v, axis=0, keepdims=True)


def onehot(index, axis, shape):
    return jnp.where(lax.broadcasted_iota(jnp.int32, shape, axis) == index, 1.0, 0.0).astype(BF16)


def block(i, size):
    return pl.ds(pl.multiple_of(i * size, size), size)


def first_kernel(feat, w_reduce, w_short, sel, conv1, sub_in, conv_short, mom):
    rows = STEP * SIDE * SIDE
    part = STEP * Q
    wide = w_short.shape[1]
    mid = w_reduce.shape[1]

    def step(g, carry):
        s1, q1, s2, q2 = carry
        x = feat[block(g, rows), :]
        c = mm(x, w_reduce[...]).astype(BF16)
        cf = c.astype(F32)
        p = mm(sel[...], c).astype(BF16)
        for k in range(4):
            conv1[k, block(g, part), :] = p[k * part : (k + 1) * part]
        sub = mm(sel[:part, :], x).astype(BF16)
        sub_in[block(g, part), :] = sub
        sh = mm(sub, w_short[...]).astype(BF16)
        conv_short[block(g, part), :] = sh
        sf = sh.astype(F32)
        return s1 + sums(cf), q1 + sums(cf * cf), s2 + sums(sf), q2 + sums(sf * sf)

    z1, z2 = jnp.zeros((1, mid), F32), jnp.zeros((1, wide), F32)
    s1, q1, s2, q2 = lax.fori_loop(0, feat.shape[0] // rows, step, (z1, z1, z2, z2))
    mom[...] = jnp.zeros_like(mom)
    mom[0:1, :mid] = s1
    mom[1:2, :mid] = q1
    mom[2:3, :] = s2
    mom[3:4, :] = q2


def act_kernel(members, conv1, tot1, gm, sm, ends, act, rim):
    mid = conv1.shape[2]
    center, inv = norm_of(tot1[...], 0, mid, members)
    for k in range(4):

        def step(i, _, k=k):
            v = (conv1[k, block(i, BLOCK), :].astype(F32) - center) * inv
            act[k, block(i, BLOCK), :] = smooth(v * gm[0:1] + sm[0:1]).astype(BF16)
            return 0

        lax.fori_loop(0, conv1.shape[1] // BLOCK, step, 0)
    count = ends.shape[0] // 2
    for k, e, lane in ((2, 0, 0), (3, 0, 1), (1, 1, 0), (3, 1, 1)):
        rim[e * count : (e + 1) * count, lane * mid : (lane + 1) * mid] = mm(
            ends[e * count : (e + 1) * count, :], act[k]
        ).astype(BF16)


def conv2_kernel(act, rim, src, w_spatial, columns, conv2, mom):
    mid = act.shape[2]
    own = act.shape[1]
    far = rim.shape[0] // 2

    def step(i, carry):
        s, q = carry
        rows = block(i, BLOCK)
        at = src[rows, :]
        top = onehot(at[:, 0:1], 1, (BLOCK, own + far))
        left = onehot(at[:, 1:2], 1, (BLOCK, own + far))
        corner = onehot(at[:, 2:3], 1, (BLOCK, own + 2 * far))

        def put(slot, v):
            columns[rows, slot * mid : (slot + 1) * mid] = v.astype(BF16)

        put(1, mm(top[:, :own], act[2]) + mm(top[:, own:], rim[:far, :mid]))
        put(2, mm(top[:, :own], act[3]) + mm(top[:, own:], rim[:far, mid:]))
        put(3, mm(left[:, :own], act[1]) + mm(left[:, own:], rim[far:, :mid]))
        put(6, mm(left[:, :own], act[3]) + mm(left[:, own:], rim[far:, mid:]))
        put(0, mm(corner[:, :own], act[3]) + mm(corner[:, own:], rim[:, mid:]))
        for slot, k in ((4, 0), (5, 1), (7, 2), (8, 3)):
            columns[rows, slot * mid : (slot + 1) * mid] = act[k, rows, :]
        c = mm(columns[rows, :], w_spatial[...]).astype(BF16)
        conv2[rows, :] = c
        cf = c.astype(F32)
        return s + sums(cf), q + sums(cf * cf)

    z = jnp.zeros((1, mid), F32)
    s, q = lax.fori_loop(0, own // BLOCK, step, (z, z))
    mom[...] = jnp.zeros_like(mom)
    mom[0:1, :mid] = s
    mom[1:2, :mid] = q


def conv3_kernel(members, conv2, tot2, gm, sm, w_expand, act2, conv3, mom):
    mid = conv2.shape[1]
    center, inv = norm_of(tot2[...], 0, mid, members)

    def step(i, carry):
        s, q = carry
        rows = block(i, BLOCK)
        v = (conv2[rows, :].astype(F32) - center) * inv
        a = smooth(v * gm[1:2] + sm[1:2]).astype(BF16)
        act2[rows, :] = a
        c = mm(a, w_expand[...]).astype(BF16)
        conv3[rows, :] = c
        cf = c.astype(F32)
        return s + sums(cf), q + sums(cf * cf)

    z = jnp.zeros((1, conv3.shape[1]), F32)
    s, q = lax.fori_loop(0, conv2.shape[0] // BLOCK, step, (z, z))
    mom[...] = jnp.zeros_like(mom)
    mom[0:1, :] = s
    mom[1:2, :] = q


def result_kernel(
    members, conv3, conv_short, tot3, tot1, gw, sw, dst, dst_t, cot, up, outgoing, mom, res
):
    wide = conv3.shape[1]
    rows_all = conv3.shape[0]
    slots = cot.shape[0]
    c3, i3 = norm_of(tot3[...], 0, wide, members)
    cs, is_ = norm_of(tot1[...], 2, wide, members)

    def step(i, carry):
        a, b, c = carry
        rows = block(i, BLOCK)
        n3 = (conv3[rows, :].astype(F32) - c3) * i3
        ns = (conv_short[rows, :].astype(F32) - cs) * is_
        summed = n3 * gw[0:1] + sw[0:1] + (ns * gw[1:2] + sw[1:2])
        res[rows, :] = smooth(summed).astype(BF16)
        picked = mm(onehot(dst[rows, :], 1, (BLOCK, slots)), cot[...])
        u = picked * slope(summed)
        up[rows, :] = u
        return a + sums(u), b + sums(u * n3), c + sums(u * ns)

    z = jnp.zeros((1, wide), F32)
    a, b, c = lax.fori_loop(0, rows_all // BLOCK, step, (z, z, z))
    mom[...] = jnp.zeros_like(mom)
    mom[0:1, :] = a
    mom[1:2, :] = b
    mom[2:3, :] = c

    def send(i, _):
        at = dst_t[...] - i * BLOCK
        outgoing[block(i, BLOCK), :] = mm(onehot(at, 0, (BLOCK, rows_all)), res[...]).astype(BF16)
        return 0

    lax.fori_loop(0, slots // BLOCK, send, 0)


def back3_kernel(
    wide_members,
    mid_members,
    up,
    conv3,
    conv_short,
    tot3,
    tot1,
    totb,
    gw,
    act2,
    sub_in,
    conv2,
    tot2,
    gm,
    sm,
    w_expand,
    dshort,
    g_expand,
    g_short,
    back2,
    mom,
    d3,
):
    wide = conv3.shape[1]
    mid = conv2.shape[1]
    rows_all = conv3.shape[0]
    c3, i3 = norm_of(tot3[...], 0, wide, wide_members)
    cs, is_ = norm_of(tot1[...], 2, wide, wide_members)
    f3, h3 = back_of(totb[...], 0, 1, gw[0:1], wide, wide_members)
    fs, hs = back_of(totb[...], 0, 2, gw[1:2], wide, wide_members)
    c2, i2 = norm_of(tot2[...], 0, mid, mid_members)

    def step(i, carry):
        s, q = carry
        rows = block(i, BLOCK)
        u = up[rows, :]
        n3 = (conv3[rows, :].astype(F32) - c3) * i3
        ns = (conv_short[rows, :].astype(F32) - cs) * is_
        d = (i3 * (gw[0:1] * u - f3 - n3 * h3)).astype(BF16)
        d3[rows, :] = d
        dshort[rows, :] = (is_ * (gw[1:2] * u - fs - ns * hs)).astype(BF16)
        n2 = (conv2[rows, :].astype(F32) - c2) * i2
        b = mm_t(d, w_expand[...]) * slope(n2 * gm[1:2] + sm[1:2])
        back2[rows, :] = b
        return s + sums(b), q + sums(b * n2)

    z = jnp.zeros((1, mid), F32)
    s, q = lax.fori_loop(0, rows_all // BLOCK, step, (z, z))
    mom[...] = jnp.zeros_like(mom)
    mom[0:1, :mid] = s
    mom[1:2, :mid] = q
    g_expand[...] = t_mm(act2[...], d3[...]).astype(BF16)

    for j in range(wide // BLOCK):
        cut = slice(j * BLOCK, (j + 1) * BLOCK)
        g_short[cut, :] = t_mm(sub_in[:, cut], dshort[...]).astype(BF16)


def back2_kernel(
    members,
    back2,
    conv2,
    tot2,
    totb,
    gm,
    columns,
    src_t,
    w_spatial,
    rims,
    g_spatial,
    planes,
    rim,
    d2,
):
    mid = conv2.shape[1]
    own = conv2.shape[0]
    far = rims // 2
    c2, i2 = norm_of(tot2[...], 0, mid, members)
    f2, h2 = back_of(totb[...], 0, 1, gm[1:2], mid, members)
    n2 = (conv2[...].astype(F32) - c2) * i2
    d2[...] = (i2 * (gm[1:2] * back2[...] - f2 - n2 * h2)).astype(BF16)
    d = d2[...]

    def part(slot):
        return mm_t(d, w_spatial[slot * mid : (slot + 1) * mid, :])

    for slot in range(9):
        cut = slice(slot * mid, (slot + 1) * mid)
        g_spatial[cut, :] = t_mm(columns[:, cut], d).astype(BF16)
    top_a, top_b = part(1).astype(BF16), part(2).astype(BF16)
    left_a, left_b = part(3).astype(BF16), part(6).astype(BF16)
    corner = part(0).astype(BF16)
    planes[0] = part(4)
    planes[1] = part(5)
    planes[2] = part(7)
    planes[3] = part(8)
    top_at, left_at, corner_at = src_t[0:1, :], src_t[1:2, :], src_t[2:3, :]

    def step(i, _):
        rows = block(i, BLOCK)
        top = onehot(top_at - i * BLOCK, 0, (BLOCK, own))
        left = onehot(left_at - i * BLOCK, 0, (BLOCK, own))
        both = onehot(corner_at - i * BLOCK, 0, (BLOCK, own))
        planes[1, rows, :] += mm(left, left_a)
        planes[2, rows, :] += mm(top, top_a)
        planes[3, rows, :] += mm(top, top_b) + mm(left, left_b) + mm(both, corner)
        return 0

    lax.fori_loop(0, own // BLOCK, step, 0)
    top = onehot(top_at - own, 0, (far, own))
    left = onehot(left_at - own, 0, (far, own))
    over = onehot(corner_at - own, 0, (far, own))
    beside = onehot(corner_at - own - far, 0, (far, own))
    rim[:far, :mid] = mm(top, top_a).astype(BF16)
    rim[:far, mid:] = (mm(top, top_b) + mm(over, corner)).astype(BF16)
    rim[far:, :mid] = mm(left, left_a).astype(BF16)
    rim[far:, mid:] = (mm(left, left_b) + mm(beside, corner)).astype(BF16)


def back1_kernel(members, planes, rim, ends, conv1, tot1, gm, sm, back1, mom):
    mid = conv1.shape[2]
    far = ends.shape[0] // 2
    center, inv = norm_of(tot1[...], 0, mid, members)
    s = q = jnp.zeros((1, mid), F32)
    for k in range(4):
        v = planes[k]
        if k >= 2:
            v = v + t_mm(ends[:far, :], rim[:far, (k - 2) * mid : (k - 1) * mid])
        if k % 2:
            lane = k // 2
            v = v + t_mm(ends[far:, :], rim[far:, lane * mid : (lane + 1) * mid])
        n = (conv1[k].astype(F32) - center) * inv
        b = v * slope(n * gm[0:1] + sm[0:1])
        back1[k] = b
        s, q = s + sums(b), q + sums(b * n)
    mom[...] = jnp.zeros_like(mom)
    mom[0:1, :mid] = s
    mom[1:2, :mid] = q


def last_kernel(
    members,
    back1,
    conv1,
    tot1,
    totb,
    gm,
    feat,
    w_reduce,
    dshort,
    w_short,
    sel_t,
    g_feat,
    g_reduce,
    total,
):
    mid = conv1.shape[2]
    rows = STEP * SIDE * SIDE
    part = STEP * Q
    center, inv = norm_of(tot1[...], 0, mid, members)
    first, second = back_of(totb[...], 0, 1, gm[0:1], mid, members)
    total[...] = jnp.zeros_like(total)

    def step(g, _):
        cuts = []
        for k in range(4):
            n = (conv1[k, block(g, part), :].astype(F32) - center) * inv
            u = back1[k, block(g, part), :]
            cuts.append((inv * (gm[0:1] * u - first - n * second)).astype(BF16))
        d = jnp.concatenate(cuts, axis=0)
        total[...] += t_mm(feat[block(g, rows), :], mm(sel_t[...], d).astype(BF16))
        short = mm_t(dshort[block(g, part), :], w_short[...])
        back = mm_t(d, w_reduce[...])
        back = jnp.concatenate([back[:part] + short, back[part:]], axis=0).astype(BF16)
        g_feat[block(g, rows), :] = mm(sel_t[...], back).astype(BF16)
        return 0

    lax.fori_loop(0, feat.shape[0] // rows, step, 0)
    g_reduce[...] = total[...].astype(BF16)


def local(kernel, outs, scratch=()):
    vmem = pl.BlockSpec(memory_space=pltpu.VMEM)

    def call(*args):
        return pl.pallas_call(
            kernel,
            out_shape=[jax.ShapeDtypeStruct(s, t) for s, t in outs],
            in_specs=[vmem] * len(args),
            out_specs=[vmem] * len(outs),
            scratch_shapes=[pltpu.VMEM(s, t) for s, t in scratch],
            compiler_params=pltpu.CompilerParams(vmem_limit_bytes=40 * 1024 * 1024),
        )(*args)

    return call


def sum_kernel(peers, x, out, slots, send, recv):
    me = lax.axis_index("space")
    barrier = pltpu.get_barrier_semaphore()
    for k in range(1, peers):
        pl.semaphore_signal(
            barrier, inc=1, device_id={"space": lax.rem(me + k, peers)}, device_id_type=MESH
        )
    slots[0] = x[...]
    pl.semaphore_wait(barrier, peers - 1)
    copies = []
    for k in range(1, peers):
        copy = pltpu.make_async_remote_copy(
            src_ref=x,
            dst_ref=slots.at[k],
            send_sem=send.at[k],
            recv_sem=recv.at[k],
            device_id={"space": lax.rem(me + k, peers)},
            device_id_type=MESH,
        )
        copy.start()
        copies.append(copy)
    for copy in copies:
        copy.wait()
    total = slots[me]
    for s in range(1, peers):
        total = total + slots[lax.rem(me - s + peers, peers)]
    out[...] = total


def slide_total(table):
    peers = lax.axis_size("space")
    vmem = pl.BlockSpec(memory_space=pltpu.VMEM)
    return pl.pallas_call(
        functools.partial(sum_kernel, peers),
        out_shape=jax.ShapeDtypeStruct(table.shape, F32),
        in_specs=[vmem],
        out_specs=vmem,
        scratch_shapes=[
            pltpu.VMEM((peers,) + table.shape, F32),
            pltpu.SemaphoreType.DMA((peers,)),
            pltpu.SemaphoreType.DMA((peers,)),
        ],
        compiler_params=pltpu.CompilerParams(collective_id=1, has_side_effects=True),
    )(table)


def share_kernel(
    groups, peers, w, vec, out, vec_out, in1, inv, mid, in2, done, in3, s1, r1, sv, rv, s2, r2, s3, r3
):
    d = lax.axis_index("dp")
    me = lax.axis_index("space")
    barrier = pltpu.get_barrier_semaphore()
    for k in range(1, groups):
        pl.semaphore_signal(
            barrier, inc=1, device_id={"dp": lax.rem(d + k, groups)}, device_id_type=MESH
        )
    for k in range(1, peers):
        pl.semaphore_signal(
            barrier, inc=1, device_id={"space": lax.rem(me + k, peers)}, device_id_type=MESH
        )
    inv[0] = vec[...]
    pl.semaphore_wait(barrier, groups + peers - 2)

    def across(k, src, dst, send, recv):
        copy = pltpu.make_async_remote_copy(
            src_ref=src,
            dst_ref=dst,
            send_sem=send.at[k],
            recv_sem=recv.at[k],
            device_id={"dp": lax.rem(d + k, groups)},
            device_id_type=MESH,
        )
        copy.start()
        return copy

    copies = []
    for k in range(1, groups):
        copies.append(across(k, w.at[lax.rem(d + k, groups)], in1.at[k], s1, r1))
        copies.append(across(k, vec, inv.at[k], sv, rv))
    for copy in copies:
        copy.wait()

    def add(i, _):
        total = w[d, i].astype(F32)
        for k in range(1, groups):
            total = total + in1[k, i].astype(F32)
        mid[i] = total.astype(BF16)
        return 0

    lax.fori_loop(0, peers, add, 0)
    copies = []
    for k in range(1, peers):
        to = lax.rem(me + k, peers)
        copy = pltpu.make_async_remote_copy(
            src_ref=mid.at[to],
            dst_ref=in2.at[k],
            send_sem=s2.at[k],
            recv_sem=r2.at[k],
            device_id={"space": to},
            device_id_type=MESH,
        )
        copy.start()
        copies.append(copy)
    total = inv[d]
    for s in range(1, groups):
        total = total + inv[lax.rem(d - s + groups, groups)]
    vec_out[...] = total
    for copy in copies:
        copy.wait()
    total = mid[me].astype(F32)
    for k in range(1, peers):
        total = total + in2[k].astype(F32)
    done[...] = total.astype(BF16)
    copies = [across(k, done, in3.at[k], s3, r3) for k in range(1, groups)]
    out[d] = done[...].astype(F32)
    for k, copy in enumerate(copies):
        copy.wait()
        out[lax.rem(d - k - 1 + groups, groups)] = in3[k + 1].astype(F32)


def share_total(w, vec):
    groups, peers = lax.axis_size("dp"), lax.axis_size("space")
    piece = w.shape[2:]
    vmem = pl.BlockSpec(memory_space=pltpu.VMEM)
    dma = pltpu.SemaphoreType.DMA
    return pl.pallas_call(
        functools.partial(share_kernel, groups, peers),
        out_shape=[
            jax.ShapeDtypeStruct((groups,) + piece, F32),
            jax.ShapeDtypeStruct(vec.shape, F32),
        ],
        in_specs=[vmem] * 2,
        out_specs=[vmem] * 2,
        scratch_shapes=[
            pltpu.VMEM(w.shape, BF16),
            pltpu.VMEM((groups,) + vec.shape, F32),
            pltpu.VMEM((peers,) + piece, BF16),
            pltpu.VMEM((peers,) + piece, BF16),
            pltpu.VMEM(piece, BF16),
            pltpu.VMEM((groups,) + piece, BF16),
            dma((groups,)),
            dma((groups,)),
            dma((groups,)),
            dma((groups,)),
            dma((peers,)),
            dma((peers,)),
            dma((groups,)),
            dma((groups,)),
        ],
        compiler_params=pltpu.CompilerParams(
            collective_id=2, has_side_effects=True, vmem_limit_bytes=24 * 1024 * 1024
        ),
    )(w, vec)


def passed_along(shard, by):
    peers = lax.axis_size("space")
    pairs = [(i, i + by) for i in range(peers) if 0 <= i + by < peers]
    return lax.ppermute(shard, "space", pairs)


def source_rows(links, me, tiles):
    own = tiles * Q
    t = jnp.arange(tiles, dtype=jnp.int32)[:, None, None]
    i = jnp.arange(HALF, dtype=jnp.int32)[None, :, None]
    j = jnp.arange(HALF, dtype=jnp.int32)[None, None, :]
    last = HALF - 1
    far = tiles * HALF

    def away(column, r, c, along, base):
        index = links[:, column][:, None, None]
        at = index - me * tiles
        here = at * Q + r * HALF + c
        there = own + base + (at + tiles) * HALF + along
        return jnp.where(index < 0, -1, jnp.where(at >= 0, here, there))

    top = jnp.where(i > 0, t * Q + (i - 1) * HALF + j, away(0, last, j, j, 0))
    left = jnp.where(j > 0, t * Q + i * HALF + j - 1, away(1, i, last, i, 0))
    corner = jnp.where(
        i > 0,
        jnp.where(
            j > 0, t * Q + (i - 1) * HALF + j - 1, away(1, i - 1, last, i - 1, far)
        ),
        jnp.where(j > 0, away(0, last, j - 1, j - 1, 0), away(2, last, last, last, 0)),
    )
    return jnp.stack([jnp.broadcast_to(x, (tiles, HALF, HALF)).reshape(own) for x in (top, left, corner)])


def plane_order():
    order = np.zeros((STEP * SIDE * SIDE, STEP * SIDE * SIDE), np.float32)
    row = 0
    for a in range(2):
        for b in range(2):
            for t in range(STEP):
                for i in range(HALF):
                    for j in range(HALF):
                        order[row, t * SIDE * SIDE + (2 * i + a) * SIDE + 2 * j + b] = 1
                        row += 1
    return order


def rim_rows(tiles):
    ends = np.zeros((2, tiles, HALF, tiles, HALF, HALF), np.float32)
    for t in range(tiles):
        for j in range(HALF):
            ends[0, t, j, t, HALF - 1, j] = 1
            ends[1, t, j, t, j, HALF - 1] = 1
    return ends.reshape(2 * tiles * HALF, tiles * Q)


def body(
    features,
    owners,
    neighbors,
    w_reduce,
    w_spatial,
    w_expand,
    w_short,
    gm,
    sm,
    gw,
    sw,
    cotangent,
):
    spaces = lax.axis_size("space")
    groups = lax.axis_size("dp")
    me = lax.axis_index("space")
    tiles = features.shape[1]
    wide = features.shape[3]
    mid = w_reduce.shape[1]
    tiles_total = tiles * spaces
    slides = features.shape[0] * groups
    capacity = cotangent.shape[1] // spaces
    slots = spaces * capacity * Q
    own = tiles * Q
    rims = 2 * tiles * HALF
    m_in = float(tiles_total * SIDE * SIDE * (mid // GROUPS))
    m_mid = float(tiles_total * Q * (mid // GROUPS))
    m_wide = float(tiles_total * Q * (wide // GROUPS))
    table = ((8, wide), F32)

    cot_home = lax.all_to_all(
        cotangent[0].reshape(spaces, capacity * Q, wide), "space", split_axis=0, concat_axis=0, tiled=True
    ).reshape(slots, wide)
    order = plane_order()
    sel, sel_t = jnp.asarray(order, BF16), jnp.asarray(order.T, BF16)
    ends = jnp.asarray(rim_rows(tiles), BF16)
    src_t = source_rows(neighbors[0], me, tiles)
    src = src_t.T
    owner_of = owners[0][:, 0]
    earlier = jnp.arange(tiles)[None, :] < jnp.arange(tiles)[:, None]
    same = (owner_of[:, None] == owner_of[None, :]) & earlier
    slot_of = owner_of * capacity + jnp.sum(same.astype(jnp.int32), axis=1)
    dst = (slot_of[:, None] * Q + jnp.arange(Q, dtype=jnp.int32)[None, :]).reshape(own)
    feat = features[0].reshape(tiles * SIDE * SIDE, wide)

    conv1, sub_in, conv_short, mom = local(
        first_kernel,
        [((4, own, mid), BF16), ((own, wide), BF16), ((own, wide), BF16), table],
    )(feat, w_reduce, w_short, sel)
    tot1 = slide_total(mom)
    act, rim = local(
        functools.partial(act_kernel, m_in), [((4, own, mid), BF16), ((rims, 2 * mid), BF16)]
    )(conv1, tot1, gm, sm, ends)
    prior = passed_along(rim, 1)
    columns, conv2, mom = local(
        conv2_kernel, [((own, 9 * mid), BF16), ((own, mid), BF16), table]
    )(act, prior, src, w_spatial)
    tot2 = slide_total(mom)
    act2, conv3, mom = local(
        functools.partial(conv3_kernel, m_mid), [((own, mid), BF16), ((own, wide), BF16), table]
    )(conv2, tot2, gm, sm, w_expand)
    tot3 = slide_total(mom)
    up, outgoing, mom = local(
        functools.partial(result_kernel, m_wide),
        [((own, wide), F32), ((slots, wide), BF16), table],
        [((own, wide), BF16)],
    )(conv3, conv_short, tot3, tot1, gw, sw, dst[:, None], dst[None, :], cot_home)
    arrived = lax.all_to_all(
        outgoing.reshape(spaces, capacity * Q, wide), "space", split_axis=0, concat_axis=0, tiled=True
    )
    block_out = arrived.reshape(1, spaces * capacity, Q, wide)
    tot3b = slide_total(mom)
    dshort, g_expand, g_short, back2, mom = local(
        functools.partial(back3_kernel, m_wide, m_mid),
        [
            ((own, wide), BF16),
            ((mid, wide), BF16),
            ((wide, wide), BF16),
            ((own, mid), F32),
            table,
        ],
        [((own, wide), BF16)],
    )(up, conv3, conv_short, tot3, tot1, tot3b, gw, act2, sub_in, conv2, tot2, gm, sm, w_expand)
    tot2b = slide_total(mom)

    def back2_entry(a, b, c, d, e, f, g, h, *rest):
        back2_kernel(m_mid, a, b, c, d, e, f, g, h, rims, *rest)

    g_spatial, planes, rim = local(
        back2_entry,
        [((9 * mid, mid), BF16), ((4, own, mid), F32), ((rims, 2 * mid), BF16)],
        [((own, mid), BF16)],
    )(back2, conv2, tot2, tot2b, gm, columns, src_t, w_spatial)
    following = passed_along(rim, -1)
    back1, mom = local(
        functools.partial(back1_kernel, m_in), [((4, own, mid), F32), table]
    )(planes, following, ends, conv1, tot1, gm, sm)
    tot1b = slide_total(mom)
    g_feat, g_reduce = local(
        functools.partial(last_kernel, m_in),
        [((tiles * SIDE * SIDE, wide), BF16), ((wide, mid), BF16)],
        [((wide, mid), F32)],
    )(back1, conv1, tot1, tot1b, gm, feat, w_reduce, dshort, w_short, sel_t)

    lanes = mid

    def cut(g):
        share = g.shape[0] // spaces
        wide_by = g.shape[1] // lanes
        g = g.reshape(spaces, share, wide_by, lanes).transpose(0, 2, 1, 3)
        return g.reshape(spaces, share * wide_by, lanes)

    parts = [cut(g) for g in (g_reduce, g_spatial, g_expand, g_short)]
    counts = [p.shape[1] for p in parts]
    piece = -(-sum(counts) // (groups * 16)) * 16
    filler = jnp.zeros((spaces, groups * piece - sum(counts), lanes), BF16)
    packed = jnp.concatenate(parts + [filler], axis=1)
    packed = packed.reshape(spaces, groups, piece, lanes).transpose(1, 0, 2, 3)
    vec = jnp.concatenate(
        [
            jnp.concatenate([tot1b[:2, :mid], tot2b[:2, :mid]], axis=1),
            jnp.zeros((2, wide - 2 * mid), F32),
        ],
        axis=1,
    )
    vec = jnp.concatenate([vec, tot3b[:3], jnp.zeros((3, wide), F32)], axis=0)
    shares, sums_dp = share_total(packed, vec)
    shares = shares.reshape(groups * piece, lanes)
    scale_in = 1.0 / math.sqrt(slides * tiles_total * SIDE * SIDE)
    scale_out = 1.0 / math.sqrt(slides * tiles_total * Q)

    def uncut(at, count, columns_by):
        g = shares[at : at + count].reshape(columns_by, count // columns_by, lanes)
        return g.transpose(1, 0, 2).reshape(count // columns_by, columns_by * lanes)

    def own_part(a):
        share = a.shape[1] // spaces
        return lax.dynamic_slice_in_dim(a, me * share, share, 1)

    at = [0]
    for c in counts:
        at.append(at[-1] + c)
    mid_scale = jnp.array([[scale_in], [scale_out]], F32)
    return (
        block_out,
        g_feat.reshape(1, tiles, SIDE * SIDE, wide),
        uncut(at[0], counts[0], 1) * scale_in,
        uncut(at[1], counts[1], 1) * scale_out,
        uncut(at[2], counts[2], wide // lanes) * scale_out,
        uncut(at[3], counts[3], wide // lanes) * scale_out,
        own_part(jnp.stack([sums_dp[1, :mid], sums_dp[1, mid : 2 * mid]])) * mid_scale,
        own_part(jnp.stack([sums_dp[0, :mid], sums_dp[0, mid : 2 * mid]])) * mid_scale,
        own_part(sums_dp[3:5]) * scale_out,
        own_part(jnp.stack([sums_dp[2], sums_dp[2]])) * scale_out,
    )


def solution(mesh):
    placed = (
        P("dp", "space", None, None),
        P("dp", "space", None),
        P("dp", "space", None),
        P(),
        P(),
        P(),
        P(),
        P(),
        P(),
        P(),
        P(),
        P("dp", "space", None, None),
    )
    return jax.shard_map(
        body,
        mesh=mesh,
        in_specs=placed,
        out_specs=(
            P("dp", "space", None, None),
            P("dp", "space", None, None),
            P("space", None),
            P("space", None),
            P("space", None),
            P("space", None),
            P(None, "space"),
            P(None, "space"),
            P(None, "space"),
            P(None, "space"),
        ),
        check_vma=False,
    )
```

time: 872 us -> 195 us (0.22)
  local copies, waits for them, and re-layouts: 357 us -> 45.9 us
  waiting for transfers between devices: 282 us -> 0.01 us
  Pallas kernels: 0 us -> 125 us
  blocking collectives: 124 us -> 0 us
  other arithmetic: 51.4 us -> 5.37 us
  matrix products: 19.8 us -> 0 us
  between operations: 15.7 us -> 1.38 us
    slice x26 -> x7, local copies, waits for them, and re-layouts: 297 us -> 1.13 us  [the longest x1 0.56 us: body(): tot2b[:2, :mid]]
    pallas_call x0 -> x16, Pallas kernels: none -> 125 us  [the longest x6 69.3 us: slide_total(): pl.pallas_call(functools.partial(sum_kernel, peers), out_shape=jax.ShapeD...]
    psum x6 -> x0, blocking collectives: 124 us -> none  [slide_total(): return lax.psum(partial_sums, 'space')]
    reduce_scatter x2 -> x0, waiting for transfers between devices: 123 us -> none  [the longest x1 61.8 us: body(): lax.psum_scatter(grad_expand_part.astype(jnp.bfloat16), 'space', scatter_...]
    unnamed x8 -> x0, waiting for transfers between devices: 116 us -> none
    psum x2 -> x0, waiting for transfers between devices: 41.8 us -> none  [the longest x1 29.6 us: body(): lax.psum(share_short.astype(jnp.bfloat16), 'dp').astype(jnp.float32)]
    scatter-add x12 -> x0, other arithmetic: 23.1 us -> none  [the longest x9 19.5 us: body(): back_pad = back_pad.at[:, offset_row:offset_row + SIDE - 1:2, offset_col:...]
    dot_general x20 -> x0, matrix products: 19.8 us -> none  [the longest x1 2.31 us: body(): jnp.dot(flat_in, w_reduce, preferred_element_type=jnp.float32)]
  transfers between devices with their start and end apart: 10 -> 4, of which waited for: 7 -> 0; matrix products, arithmetic and copies ran while one was open for 41% -> 6% of each run, Pallas kernels for 0% -> 41%
where the time goes in v1:
time: 195 us; the launch traced here: 193 us
  Pallas kernels  125 us (64%)
  local copies, waits for them, and re-layouts  45.9 us (24%)
  starting transfers between devices  16.1 us (8%)
  other arithmetic  5.37 us (3%)
    pallas_call x6, Pallas kernels, slide_total(): pl.pallas_call(functools.partial(sum_kernel, peers), out_shape=jax.ShapeD...  69.3 us
    unnamed x128, local copies, waits for them, and re-layouts  39.8 us
    pallas_call x9, Pallas kernels, call(): pl.pallas_call(kernel, out_shape=[jax.ShapeDtypeStruct(s, t) for s, t in...  30.8 us
    pallas_call x1, Pallas kernels, share_total(): pl.pallas_call(functools.partial(share_kernel, groups, peers), out_shape=...  24.6 us
    all_to_all x1, starting transfers between devices, body(): lax.all_to_all(outgoing.reshape(spaces, capacity * Q, wide), 'space', spl...  6.62 us
    ppermute x2, starting transfers between devices, passed_along(): return lax.ppermute(shard, 'space', pairs)  5.03 us
    all_to_all x1, starting transfers between devices, body(): lax.all_to_all(cotangent[0].reshape(spaces, capacity * Q, wide), 'space',...  4.43 us
  transfers between devices with their start and end apart: 4, of which 0 were waited for; matrix products, arithmetic and copies ran while one was open for 6% of the time, Pallas kernels for 41%

profile of v1, /device:TPU:0, one launch (start us, length us, event | category | flops | bytes accessed | tf_op | source)
XLA Modules:
  0.0 193.4 jit_solution(3246795591225996497)
XLA Ops:
  0.7 1.6 copy-done
  2.2 1.0 copy-done.2
  3.3 0.9 copy-done.17
  4.2 0.9 copy-done.35
  5.1 3.9 %shard_map.231 = (bf16[4,512,128]{2,1,0:T(8,128)(2,1)S(1)}, bf16[512,512]{1,0:T(8,128)(2,1)S(1)}, bf16[512,512]{1,0:T(8,128)(2,1)S(1)}, f32[8,512]{1,0:T(8,128)S(1)}) custom-call(bf16[2048,512]{1,0:T(8,128)(2,1)S(1)} %bitcast.58, bf16[512,128]{1,0:T(8,128)(2,1)S(1)} %copy-done.17, bf16[512,512]{1,0:T(8,128)(2,1)S(1)} %copy-done.2, ...), custom_call_target="tpu_custom_call" | custom-call | tf_op jit(solution)/shard_map/pallas_call | solution.py:415
  9.0 0.8 copy-done.21
  10.4 10.6 %shard_map.232.tot1 = f32[8,512]{1,0:T(8,128)} custom-call(f32[8,512]{1,0:T(8,128)} %copy-done.50), custom_call_target="tpu_custom_call" | custom-call | tf_op jit(solution)/shard_map/pallas_call | solution.py:459
  21.0 0.7 copy-done.15
  21.7 1.8 shard_map.233
  23.6 3.7 %collective-permute-start = (bf16[256,256]{1,0:T(8,128)(2,1)}, bf16[256,256]{1,0:T(8,128)(2,1)S(1)}, u32[]{:S(2)}, u32[]{:S(2)}) collective-permute-start(bf16[256,256]{1,0:T(8,128)(2,1)} %get-tuple-element.42), channel_id=1, source_target_pairs={{0,1},{1,2},{2,3},{3,4},{4,5},{5,6},{6,7},{8,9},{9,10},{10,11},{11... | collective-permute-start | bytes 393224 | tf_op jit(solution)/shard_map/ppermute | solution.py:585
  27.3 4.4 %all-to-all-start = ((bf16[8,128,512]{2,1,0:T(8,128)(2,1)}), bf16[8,128,512]{2,1,0:T(8,128)(2,1)S(1)}, u32[]{:S(2)}, u32[]{:S(2)}) async-start(bf16[8,128,512]{2,1,0:T(8,128)(2,1)} %bitcast.69), calls=%async_computation | async-start | bytes 2097152 | tf_op jit(solution)/shard_map/all_to_all | solution.py:668
  33.6 0.9 convert_reduce_fusion
  34.5 0.7 add_multiply_fusion
  35.3 0.9 add.516.dst
  36.4 0.6 copy-done.31
  37.1 1.0 copy-done.20
  38.1 0.9 copy-done.32
  39.0 2.7 %shard_map.234 = (bf16[512,1152]{1,0:T(8,128)(2,1)S(1)}, bf16[512,128]{1,0:T(8,128)(2,1)S(1)}, f32[8,512]{1,0:T(8,128)S(1)}) custom-call(bf16[4,512,128]{2,1,0:T(8,128)(2,1)S(1)} %copy-done.20, bf16[256,256]{1,0:T(8,128)(2,1)S(1)} %copy-done.32, s32[512,3]{1,0:T(8,128)S(1)} %copy.36.src, bf16[1152,128]{1,0:T(8,128)(2,1)S(1)} %copy-done.6), custom_call_target="tpu_custom_call" | custom-call | tf_op jit(solution)/shard_map/pallas_call | solution.py:415
  41.7 1.0 copy-done.4
  43.3 16.6 %shard_map.235.tot2.c = f32[8,512]{1,0:T(8,128)} custom-call(f32[8,512]{1,0:T(8,128)} %copy-done.48), custom_call_target="tpu_custom_call" | custom-call | tf_op jit(solution)/shard_map/pallas_call | solution.py:459
  59.9 0.7 copy-done.28
  60.6 1.0 shard_map.236
  61.7 0.6 copy-done.36
  62.9 7.9 %shard_map.237.tot3 = f32[8,512]{1,0:T(8,128)} custom-call(f32[8,512]{1,0:T(8,128)} %copy-done.52), custom_call_target="tpu_custom_call" | custom-call | tf_op jit(solution)/shard_map/pallas_call | solution.py:459
  70.9 0.9 copy-done.14
  71.9 0.7 copy-done.29
  72.6 5.7 %shard_map.238 = (f32[512,512]{1,0:T(8,128)S(1)}, bf16[1024,512]{1,0:T(8,128)(2,1)}, f32[8,512]{1,0:T(8,128)S(1)}) custom-call(bf16[512,512]{1,0:T(8,128)(2,1)S(1)} %get-tuple-element.45.conv3, bf16[512,512]{1,0:T(8,128)(2,1)S(1)} %get-tuple-element.46.conv_short, f32[8,512]{1,0:T(8,128)S(1)} %copy-done.29, f32[8,512]{1,0:T(8,128)S(1)} %copy-done.16, ...), custom_call_target="tpu_custom_call" | custom-call | tf_op jit(solution)/shard_map/pallas_call | solution.py:415
  78.3 1.0 copy-done.10
  79.8 8.0 %shard_map.239.totb = f32[8,512]{1,0:T(8,128)} custom-call(f32[8,512]{1,0:T(8,128)} %copy-done.49), custom_call_target="tpu_custom_call" | custom-call | tf_op jit(solution)/shard_map/pallas_call | solution.py:459
  87.8 1.2 copy-done.11
  89.0 1.0 copy-done.22
  90.1 0.9 copy-done.37
  91.0 0.7 copy-done.38
  91.7 3.0 %shard_map.240 = (bf16[512,512]{1,0:T(8,128)(2,1)S(1)}, bf16[128,512]{1,0:T(8,128)(2,1)S(1)}, bf16[512,512]{1,0:T(8,128)(2,1)S(1)}, f32[512,128]{1,0:T(8,128)S(1)}, f32[8,512]{1,0:T(8,128)S(1)}) custom-call(f32[512,512]{1,0:T(8,128)S(1)} %copy-done.11, bf16[512,512]{1,0:T(8,128)(2,1)S(1)} %get-tuple-element.45.conv3, ...), custom_call_target="tpu_custom_call" | custom-call | tf_op jit(solution)/shard_map/pallas_call | solution.py:415
  94.7 0.8 copy-done.23
  96.1 8.6 %shard_map.241.d = f32[8,512]{1,0:T(8,128)} custom-call(f32[8,512]{1,0:T(8,128)} %copy-done.47), custom_call_target="tpu_custom_call" | custom-call | tf_op jit(solution)/shard_map/pallas_call | solution.py:459
  104.8 1.3 copy-done.5
  106.0 0.7 copy-done.39
  106.7 3.4 %shard_map.242 = (bf16[1152,128]{1,0:T(8,128)(2,1)S(1)}, f32[4,512,128]{2,1,0:T(8,128)S(1)}, bf16[256,256]{1,0:T(8,128)(2,1)}) custom-call(f32[512,128]{1,0:T(8,128)S(1)} %get-tuple-element.53.a, bf16[512,128]{1,0:T(8,128)(2,1)S(1)} %get-tuple-element.43.conv2.b, f32[8,512]{1,0:T(8,128)S(1)} %copy-done.28, f32[8,512]{1,0:T(8,128)S(1)} %copy-done.39, ...), custom_call_target="tpu_custom_call" | custom-call | tf_op jit(solution)/shard_map/pallas_call | solution.py:415
  110.1 1.0 copy-done.8
  111.1 0.7 copy-done.26
  111.8 1.3 collective-permute-start.1
  114.3 6.6 %all-to-all-start.1 = ((bf16[8,128,512]{2,1,0:T(8,128)(2,1)}), bf16[8,128,512]{2,1,0:T(8,128)(2,1)}, u32[]{:S(2)}, u32[]{:S(2)}) async-start(bf16[8,128,512]{2,1,0:T(8,128)(2,1)} %bitcast.15), calls=%async_computation.1 | async-start | bytes 2097152 | tf_op jit(solution)/shard_map/all_to_all | solution.py:705
  120.9 0.7 copy.38
  121.7 0.9 copy.39
  122.7 0.7 copy-done.33
  123.3 1.2 copy-done.9
  124.5 0.9 copy-done.34
  125.4 0.7 copy-done.42
  126.1 0.7 copy-done.46
  126.8 1.0 shard_map.243
  127.8 1.0 copy-done.12
  129.4 17.6 %shard_map.244.totb = f32[8,512]{1,0:T(8,128)} custom-call(f32[8,512]{1,0:T(8,128)} %copy-done.51), custom_call_target="tpu_custom_call" | custom-call | tf_op jit(solution)/shard_map/pallas_call | solution.py:459
  147.1 1.2 copy-done.13
  148.3 1.0 copy-done.24
  149.3 0.9 copy-done.30
  150.2 0.7 copy-done.40
  151.0 0.7 copy-done.43
  151.6 8.3 %shard_map.245 = (bf16[2048,512]{1,0:T(8,128)(2,1)}, bf16[512,128]{1,0:T(8,128)(2,1)S(1)}) custom-call(f32[4,512,128]{2,1,0:T(8,128)S(1)} %copy-done.13, bf16[4,512,128]{2,1,0:T(8,128)(2,1)S(1)} %get-tuple-element.39.conv1, f32[8,512]{1,0:T(8,128)S(1)} %copy-done.16, f32[8,512]{1,0:T(8,128)S(1)} %copy-done.40, f32[2,128]{1,0:T(2,128)S(1)} %copy-done.43, ...), custom_call_target="tpu_custom_call" | custom-call | tf_op jit(solution)/shard_map/pallas_call | solution.py:415
  160.0 0.9 copy-done.54
  161.9 24.6 %shard_map.246 = (f32[4,144,128]{2,1,0:T(8,128)S(1)}, f32[8,512]{1,0:T(8,128)S(1)}) custom-call(bf16[4,8,144,128]{3,2,1,0:T(8,128)(2,1)S(1)} %bitcast.60, f32[8,512]{1,0:T(8,128)S(1)} %maximum_maximum_fusion.vec), custom_call_target="tpu_custom_call" | custom-call | tf_op jit(solution)/shard_map/pallas_call | solution.py:552
  187.8 0.7 copy.51
  189.8 0.6 fusion.2
  191.1 2.3 %copy.59 = bf16[1,64,16,512]{3,2,1,0:T(8,128)(2,1)} copy(bf16[1,64,16,512]{3,2,1,0:T(8,128)(2,1)} %bitcast.16) | data formatting | bytes 2097152
  (148 shorter events, 11.3 us)
Async XLA Ops:
  0.6 1.6 copy-start
  2.2 1.0 copy-start.2
  3.3 0.9 copy-start.17
  4.2 0.9 copy-start.35
  5.1 15.9 %copy-start.7 = (bf16[256,512]{1,0:T(8,128)(2,1)S(1)}, bf16[256,512]{1,0:T(8,128)(2,1)}, u32[]{:S(2)}) copy-start(bf16[256,512]{1,0:T(8,128)(2,1)} %constant.17.clone.ends) | copy-start | bytes 786436
  5.1 15.9 %copy-start.41 = (f32[2,128]{1,0:T(2,128)S(1)}, f32[2,128]{1,0:T(2,128)}, u32[]{:S(2)}) copy-start(f32[2,128]{1,0:T(2,128)} %gm.9) | copy-start | bytes 3076
  5.1 15.9 %copy-start.45 = (f32[2,128]{1,0:T(2,128)S(1)}, f32[2,128]{1,0:T(2,128)}, u32[]{:S(2)}) copy-start(f32[2,128]{1,0:T(2,128)} %sm.7) | copy-start | bytes 3076
  9.0 0.8 copy-start.21
  9.8 0.6 copy-start.50
  21.0 0.7 copy-start.15
  23.6 8.8 %copy-start.19 = (bf16[4,512,128]{2,1,0:T(8,128)(2,1)}, bf16[4,512,128]{2,1,0:T(8,128)(2,1)S(1)}, u32[]{:S(2)}) copy-start(bf16[4,512,128]{2,1,0:T(8,128)(2,1)S(1)} %get-tuple-element.41.act) | copy-start | bytes 1572868
  23.6 8.2 %copy-start.57 = (s32[1,32,3]{1,0,2:T(1,128)S(1)}, s32[1,32,3]{1,0,2:T(1,128)}, u32[]{:S(2)}) copy-start(s32[1,32,3]{1,0,2:T(1,128)} %param.18) | copy-start | bytes 1156
  23.6 12.9 %collective-permute-start = (bf16[256,256]{1,0:T(8,128)(2,1)}, bf16[256,256]{1,0:T(8,128)(2,1)S(1)}, u32[]{:S(2)}, u32[]{:S(2)}) collective-permute-start(bf16[256,256]{1,0:T(8,128)(2,1)} %get-tuple-element.42), channel_id=1, source_target_pairs={{0,1},{1,2},{2,3},{3,4},{4,5},{5,6},{6,7},{8,9},{9,10},{10,11},{11... | collective-permute-start | bytes 393224 | tf_op jit(solution)/shard_map/ppermute | solution.py:585
  27.3 43.6 %all-to-all-start = ((bf16[8,128,512]{2,1,0:T(8,128)(2,1)}), bf16[8,128,512]{2,1,0:T(8,128)(2,1)S(1)}, u32[]{:S(2)}, u32[]{:S(2)}) async-start(bf16[8,128,512]{2,1,0:T(8,128)(2,1)} %bitcast.69), calls=%async_computation | async-start | bytes 2097152 | tf_op jit(solution)/shard_map/all_to_all | solution.py:668
  31.7 5.3 %copy-start.6 = (bf16[1152,128]{1,0:T(8,128)(2,1)S(1)}, bf16[1152,128]{1,0:T(8,128)(2,1)}, u32[]{:S(2)}) copy-start(bf16[1152,128]{1,0:T(8,128)(2,1)} %h.1) | copy-start | bytes 884740
  32.8 27.1 %copy-start.25 = (bf16[128,512]{1,0:T(8,128)(2,1)S(1)}, bf16[128,512]{1,0:T(8,128)(2,1)}, u32[]{:S(2)}) copy-start(bf16[128,512]{1,0:T(8,128)(2,1)} %w_expand.3) | copy-start | bytes 393220
  33.4 37.5 %copy-start.16 = (f32[8,512]{1,0:T(8,128)S(1)}, f32[8,512]{1,0:T(8,128)}, u32[]{:S(2)}) copy-start(f32[8,512]{1,0:T(8,128)} %shard_map.232.tot1) | copy-start | bytes 49156
  33.4 37.5 %copy-start.44 = (f32[2,512]{1,0:T(2,128)S(1)}, f32[2,512]{1,0:T(2,128)}, u32[]{:S(2)}) copy-start(f32[2,512]{1,0:T(2,128)} %gw.3) | copy-start | bytes 12292
  33.4 37.5 %copy-start.53 = (f32[2,512]{1,0:T(2,128)S(1)}, f32[2,512]{1,0:T(2,128)}, u32[]{:S(2)}) copy-start(f32[2,512]{1,0:T(2,128)} %sw.1) | copy-start | bytes 12292
  36.4 0.7 copy-start.31
  37.1 1.0 copy-start.20
  38.1 0.9 copy-start.32
  41.7 1.0 copy-start.4
  42.7 0.6 copy-start.48
  59.9 0.7 copy-start.28
  61.7 0.7 copy-start.36
  62.3 0.6 copy-start.52
  70.9 1.0 copy-start.14
  71.9 0.7 copy-start.29
  78.3 1.0 copy-start.10
  79.2 0.6 copy-start.49
  87.8 1.2 copy-start.11
  89.0 1.0 copy-start.22
  90.1 0.9 copy-start.37
  91.0 0.7 copy-start.38
  94.7 0.8 copy-start.23
  95.5 0.6 copy-start.47
  104.7 1.3 copy-start.5
  106.0 0.7 copy-start.39
  110.1 1.0 copy-start.8
  111.1 0.7 copy-start.26
  111.8 10.9 %collective-permute-start.1 = (bf16[256,256]{1,0:T(8,128)(2,1)}, bf16[256,256]{1,0:T(8,128)(2,1)S(1)}, u32[]{:S(2)}, u32[]{:S(2)}) collective-permute-start(bf16[256,256]{1,0:T(8,128)(2,1)} %get-tuple-element.57), channel_id=1, source_target_pairs={{1,0},{2,1},{3,2},{4,3},{5,4},{6,5},{7,6},{9,8},{10,9},{11,10},{12... | collective-permute-start | bytes 393224 | tf_op jit(solution)/shard_map/ppermute | solution.py:585
  114.3 76.9 %all-to-all-start.1 = ((bf16[8,128,512]{2,1,0:T(8,128)(2,1)}), bf16[8,128,512]{2,1,0:T(8,128)(2,1)}, u32[]{:S(2)}, u32[]{:S(2)}) async-start(bf16[8,128,512]{2,1,0:T(8,128)(2,1)} %bitcast.15), calls=%async_computation.1 | async-start | bytes 2097152 | tf_op jit(solution)/shard_map/all_to_all | solution.py:705
  121.7 25.3 %copy-start.1 = (bf16[1,32,64,512]{3,2,1,0:T(8,128)(2,1)S(1)}, bf16[1,32,64,512]{3,2,1,0:T(8,128)(2,1)}, u32[]{:S(2)}) copy-start(bf16[1,32,64,512]{3,2,1,0:T(8,128)(2,1)} %param.16) | copy-start | bytes 6291460
  122.7 24.4 %copy-start.3 = (bf16[512,512]{1,0:T(8,128)(2,1)S(1)}, bf16[512,512]{1,0:T(8,128)(2,1)}, u32[]{:S(2)}) copy-start(bf16[512,512]{1,0:T(8,128)(2,1)} %w_short.3) | copy-start | bytes 1572868
  122.7 0.7 copy-start.33
  123.3 1.2 copy-start.9
  124.5 0.9 copy-start.34
  125.4 0.7 copy-start.42
  126.1 0.7 copy-start.46
  126.8 20.3 %copy-start.18 = (bf16[512,128]{1,0:T(8,128)(2,1)S(1)}, bf16[512,128]{1,0:T(8,128)(2,1)}, u32[]{:S(2)}) copy-start(bf16[512,128]{1,0:T(8,128)(2,1)} %w_reduce.3) | copy-start | bytes 393220
  127.8 1.0 copy-start.12
  147.1 1.2 copy-start.13
  148.3 1.0 copy-start.24
  149.3 0.9 copy-start.30
  150.2 0.7 copy-start.40
  151.0 0.7 copy-start.43
  151.6 8.3 %copy-start.27 = (bf16[1152,128]{1,0:T(8,128)(2,1)S(1)}, bf16[1152,128]{1,0:T(8,128)(2,1)}, u32[]{:S(2)}) copy-start(bf16[1152,128]{1,0:T(8,128)(2,1)} %copy-done.26) | copy-start | bytes 884740
  151.6 8.4 %copy-start.55 = (bf16[8,16,4,128]{3,1,2,0:T(8,128)(2,1)S(1)}, bf16[8,16,4,128]{3,1,2,0:T(8,128)(2,1)}, u32[]{:S(2)}) copy-start(bf16[8,16,4,128]{3,1,2,0:T(8,128)(2,1)} %copy.38) | copy-start | bytes 393220
  159.9 1.0 copy-start.54
  161.1 0.7 slice-start
  161.1 0.7 copy-start.56
  161.1 0.7 copy-start.58
  161.2 28.6 %copy-start.59 = (f32[2]{0:T(128)S(1)}, f32[2]{0:T(128)}, u32[]{:S(2)}) copy-start(f32[2]{0:T(128)} %constant.76) | copy-start | bytes 28
  (1 other events, 0.6 us)

commit v2 on v1

--- a/solution.py
+++ b/solution.py
@@ -82,7 +82,8 @@
 
 
 def block(i, size):
-    return pl.ds(pl.multiple_of(i * size, size), size)
+    start = i * size
+    return pl.ds(start if isinstance(start, int) else pl.multiple_of(start, size), size)
 
 
 def first_kernel(feat, w_reduce, w_short, sel, conv1, sub_in, conv_short, mom):
@@ -408,66 +409,135 @@
     g_reduce[...] = total[...].astype(BF16)
 
 
-def local(kernel, outs, scratch=()):
-    vmem = pl.BlockSpec(memory_space=pltpu.VMEM)
-
-    def call(*args):
-        return pl.pallas_call(
-            kernel,
-            out_shape=[jax.ShapeDtypeStruct(s, t) for s, t in outs],
-            in_specs=[vmem] * len(args),
-            out_specs=[vmem] * len(outs),
-            scratch_shapes=[pltpu.VMEM(s, t) for s, t in scratch],
-            compiler_params=pltpu.CompilerParams(vmem_limit_bytes=40 * 1024 * 1024),
-        )(*args)
-
-    return call
-
-
-def sum_kernel(peers, x, out, slots, send, recv):
+def whole_kernel(members, peers, *refs):
+    m_in, m_mid, m_wide = members
+    (feat, cot, src, src_t, dst, dst_t, w_reduce, w_spatial, w_expand, w_short, gm, sm, gw, sw) = refs[:14]
+    sel, sel_t, ends = refs[14:17]
+    g_feat, landed, g_reduce, g_spatial, g_expand, g_short, tot = refs[17:24]
+    (conv1, sub_in, conv_short, act, rim, prior, columns, conv2, act2, conv3) = refs[24:34]
+    (up, outgoing, res, dshort, back2, d3, d2, planes, rim_b, following, back1) = refs[34:45]
+    total, home, moms, slots = refs[45:49]
+    sum_send, sum_recv, cot_send, cot_recv, out_send, out_recv, rim_send, rim_recv = refs[49:]
     me = lax.axis_index("space")
     barrier = pltpu.get_barrier_semaphore()
     for k in range(1, peers):
         pl.semaphore_signal(
             barrier, inc=1, device_id={"space": lax.rem(me + k, peers)}, device_id_type=MESH
         )
-    slots[0] = x[...]
     pl.semaphore_wait(barrier, peers - 1)
-    copies = []
-    for k in range(1, peers):
+
+    def send(by, source, target, out_sem, in_sem):
         copy = pltpu.make_async_remote_copy(
-            src_ref=x,
-            dst_ref=slots.at[k],
-            send_sem=send.at[k],
-            recv_sem=recv.at[k],
-            device_id={"space": lax.rem(me + k, peers)},
+            src_ref=source,
+            dst_ref=target,
+            send_sem=out_sem,
+            recv_sem=in_sem,
+            device_id={"space": lax.rem(me + by, peers)},
             device_id_type=MESH,
         )
         copy.start()
-        copies.append(copy)
-    for copy in copies:
+        return copy
+
+    def slide_total(n):
+        copies = [
+            send(k, moms.at[n], slots.at[n, k], sum_send.at[n, k], sum_recv.at[n, k])
+            for k in range(1, peers)
+        ]
+        slots[n, 0] = moms[n]
+        for copy in copies:
+            copy.wait()
+        sum_of = slots[n, me]
+        for s in range(1, peers):
+            sum_of = sum_of + slots[n, lax.rem(me - s + peers, peers)]
+        tot[n] = sum_of
+
+    rows = cot.shape[1]
+    cot_copies = [
+        send(k, cot.at[lax.rem(me + k, peers)], home.at[block(k, rows)], cot_send.at[k], cot_recv.at[k])
+        for k in range(1, peers)
+    ]
+    first_kernel(feat, w_reduce, w_short, sel, conv1, sub_in, conv_short, moms.at[0])
+    slide_total(0)
+    act_kernel(m_in, conv1, tot.at[0], gm, sm, ends, act, rim)
+    send(1, rim, prior, rim_send.at[0], rim_recv.at[0]).wait()
+    conv2_kernel(act, prior, src, w_spatial, columns, conv2, moms.at[1])
+    slide_total(1)
+    conv3_kernel(m_mid, conv2, tot.at[1], gm, sm, w_expand, act2, conv3, moms.at[2])
+    slide_total(2)
+    home[:rows, :] = cot[me]
+    for copy in cot_copies:
         copy.wait()
-    total = slots[me]
-    for s in range(1, peers):
-        total = total + slots[lax.rem(me - s + peers, peers)]
-    out[...] = total
-
-
-def slide_total(table):
-    peers = lax.axis_size("space")
-    vmem = pl.BlockSpec(memory_space=pltpu.VMEM)
-    return pl.pallas_call(
-        functools.partial(sum_kernel, peers),
-        out_shape=jax.ShapeDtypeStruct(table.shape, F32),
-        in_specs=[vmem],
-        out_specs=vmem,
-        scratch_shapes=[
-            pltpu.VMEM((peers,) + table.shape, F32),
-            pltpu.SemaphoreType.DMA((peers,)),
-            pltpu.SemaphoreType.DMA((peers,)),
-        ],
-        compiler_params=pltpu.CompilerParams(collective_id=1, has_side_effects=True),
-    )(table)
+    result_kernel(
+        m_wide, conv3, conv_short, tot.at[2], tot.at[0], gw, sw, dst, dst_t, home, up, outgoing, moms.at[3], res
+    )
+    out_copies = [
+        send(k, outgoing.at[block(k, rows)], landed.at[me], out_send.at[k], out_recv.at[k])
+        for k in range(1, peers)
+    ]
+    landed[me] = outgoing[:rows, :]
+    slide_total(3)
+    back3_kernel(
+        m_wide,
+        m_mid,
+        up,
+        conv3,
+        conv_short,
+        tot.at[2],
+        tot.at[0],
+        tot.at[3],
+        gw,
+        act2,
+        sub_in,
+        conv2,
+        tot.at[1],
+        gm,
+        sm,
+        w_expand,
+        dshort,
+        g_expand,
+        g_short,
+        back2,
+        moms.at[4],
+        d3,
+    )
+    slide_total(4)
+    back2_kernel(
+        m_mid,
+        back2,
+        conv2,
+        tot.at[1],
+        tot.at[4],
+        gm,
+        columns,
+        src_t,
+        w_spatial,
+        ends.shape[0],
+        g_spatial,
+        planes,
+        rim_b,
+        d2,
+    )
+    send(peers - 1, rim_b, following, rim_send.at[1], rim_recv.at[1]).wait()
+    back1_kernel(m_in, planes, following, ends, conv1, tot.at[0], gm, sm, back1, moms.at[5])
+    slide_total(5)
+    last_kernel(
+        m_in,
+        back1,
+        conv1,
+        tot.at[0],
+        tot.at[5],
+        gm,
+        feat,
+        w_reduce,
+        dshort,
+        w_short,
+        sel_t,
+        g_feat,
+        g_reduce,
+        total,
+    )
+    for copy in out_copies:
+        copy.wait()
 
 
 def share_kernel(
@@ -579,12 +649,6 @@
     )(w, vec)
 
 
-def passed_along(shard, by):
-    peers = lax.axis_size("space")
-    pairs = [(i, i + by) for i in range(peers) if 0 <= i + by < peers]
-    return lax.ppermute(shard, "space", pairs)
-
-
 def source_rows(links, me, tiles):
     own = tiles * Q
     t = jnp.arange(tiles, dtype=jnp.int32)[:, None, None]
@@ -663,11 +727,6 @@
     m_in = float(tiles_total * SIDE * SIDE * (mid // GROUPS))
     m_mid = float(tiles_total * Q * (mid // GROUPS))
     m_wide = float(tiles_total * Q * (wide // GROUPS))
-    table = ((8, wide), F32)
-
-    cot_home = lax.all_to_all(
-        cotangent[0].reshape(spaces, capacity * Q, wide), "space", split_axis=0, concat_axis=0, tiled=True
-    ).reshape(slots, wide)
     order = plane_order()
     sel, sel_t = jnp.asarray(order, BF16), jnp.asarray(order.T, BF16)
     ends = jnp.asarray(rim_rows(tiles), BF16)
@@ -676,68 +735,85 @@
     owner_of = owners[0][:, 0]
     earlier = jnp.arange(tiles)[None, :] < jnp.arange(tiles)[:, None]
     same = (owner_of[:, None] == owner_of[None, :]) & earlier
-    slot_of = owner_of * capacity + jnp.sum(same.astype(jnp.int32), axis=1)
-    dst = (slot_of[:, None] * Q + jnp.arange(Q, dtype=jnp.int32)[None, :]).reshape(own)
+    rank_of = jnp.sum(same.astype(jnp.int32), axis=1)
+
+    def rows_of(block_of):
+        first = (lax.rem(block_of + spaces, spaces) * capacity + rank_of) * Q
+        return (first[:, None] + jnp.arange(Q, dtype=jnp.int32)[None, :]).reshape(own)
+
+    dst = rows_of(me - owner_of)[:, None]
+    dst_t = rows_of(owner_of - me)[None, :]
     feat = features[0].reshape(tiles * SIDE * SIDE, wide)
-
-    conv1, sub_in, conv_short, mom = local(
-        first_kernel,
-        [((4, own, mid), BF16), ((own, wide), BF16), ((own, wide), BF16), table],
-    )(feat, w_reduce, w_short, sel)
-    tot1 = slide_total(mom)
-    act, rim = local(
-        functools.partial(act_kernel, m_in), [((4, own, mid), BF16), ((rims, 2 * mid), BF16)]
-    )(conv1, tot1, gm, sm, ends)
-    prior = passed_along(rim, 1)
-    columns, conv2, mom = local(
-        conv2_kernel, [((own, 9 * mid), BF16), ((own, mid), BF16), table]
-    )(act, prior, src, w_spatial)
-    tot2 = slide_total(mom)
-    act2, conv3, mom = local(
-        functools.partial(conv3_kernel, m_mid), [((own, mid), BF16), ((own, wide), BF16), table]
-    )(conv2, tot2, gm, sm, w_expand)
-    tot3 = slide_total(mom)
-    up, outgoing, mom = local(
-        functools.partial(result_kernel, m_wide),
-        [((own, wide), F32), ((slots, wide), BF16), table],
-        [((own, wide), BF16)],
-    )(conv3, conv_short, tot3, tot1, gw, sw, dst[:, None], dst[None, :], cot_home)
-    arrived = lax.all_to_all(
-        outgoing.reshape(spaces, capacity * Q, wide), "space", split_axis=0, concat_axis=0, tiled=True
-    )
-    block_out = arrived.reshape(1, spaces * capacity, Q, wide)
-    tot3b = slide_total(mom)
-    dshort, g_expand, g_short, back2, mom = local(
-        functools.partial(back3_kernel, m_wide, m_mid),
-        [
-            ((own, wide), BF16),
-            ((mid, wide), BF16),
-            ((wide, wide), BF16),
-            ((own, mid), F32),
-            table,
-        ],
-        [((own, wide), BF16)],
-    )(up, conv3, conv_short, tot3, tot1, tot3b, gw, act2, sub_in, conv2, tot2, gm, sm, w_expand)
-    tot2b = slide_total(mom)
-
-    def back2_entry(a, b, c, d, e, f, g, h, *rest):
-        back2_kernel(m_mid, a, b, c, d, e, f, g, h, rims, *rest)
-
-    g_spatial, planes, rim = local(
-        back2_entry,
-        [((9 * mid, mid), BF16), ((4, own, mid), F32), ((rims, 2 * mid), BF16)],
-        [((own, mid), BF16)],
-    )(back2, conv2, tot2, tot2b, gm, columns, src_t, w_spatial)
-    following = passed_along(rim, -1)
-    back1, mom = local(
-        functools.partial(back1_kernel, m_in), [((4, own, mid), F32), table]
-    )(planes, following, ends, conv1, tot1, gm, sm)
-    tot1b = slide_total(mom)
-    g_feat, g_reduce = local(
-        functools.partial(last_kernel, m_in),
-        [((tiles * SIDE * SIDE, wide), BF16), ((wide, mid), BF16)],
-        [((wide, mid), F32)],
-    )(back1, conv1, tot1, tot1b, gm, feat, w_reduce, dshort, w_short, sel_t)
+    cot = cotangent[0].reshape(spaces, capacity * Q, wide)
+    vmem = pl.BlockSpec(memory_space=pltpu.VMEM)
+    outs = [
+        ((tiles * SIDE * SIDE, wide), BF16),
+        ((spaces, capacity * Q, wide), BF16),
+        ((wide, mid), BF16),
+        ((9 * mid, mid), BF16),
+        ((mid, wide), BF16),
+        ((wide, wide), BF16),
+        ((6, 8, wide), F32),
+    ]
+    scratch = [
+        ((4, own, mid), BF16),
+        ((own, wide), BF16),
+        ((own, wide), BF16),
+        ((4, own, mid), BF16),
+        ((rims, 2 * mid), BF16),
+        ((rims, 2 * mid), BF16),
+        ((own, 9 * mid), BF16),
+        ((own, mid), BF16),
+        ((own, mid), BF16),
+        ((own, wide), BF16),
+        ((own, wide), F32),
+        ((slots, wide), BF16),
+        ((own, wide), BF16),
+        ((own, wide), BF16),
+        ((own, mid), F32),
+        ((own, wide), BF16),
+        ((own, mid), BF16),
+        ((4, own, mid), F32),
+        ((rims, 2 * mid), BF16),
+        ((rims, 2 * mid), BF16),
+        ((4, own, mid), F32),
+        ((wide, mid), F32),
+        ((slots, wide), BF16),
+        ((6, 8, wide), F32),
+        ((6, spaces, 8, wide), F32),
+    ]
+    dma = pltpu.SemaphoreType.DMA
+    semaphores = [dma((6, spaces))] * 2 + [dma((spaces,))] * 4 + [dma((2,))] * 2
+    g_feat, landed, g_reduce, g_spatial, g_expand, g_short, tot = pl.pallas_call(
+        functools.partial(whole_kernel, (m_in, m_mid, m_wide), spaces),
+        out_shape=[jax.ShapeDtypeStruct(a, t) for a, t in outs],
+        in_specs=[vmem] * 17,
+        out_specs=[vmem] * len(outs),
+        scratch_shapes=[pltpu.VMEM(a, t) for a, t in scratch] + semaphores,
+        compiler_params=pltpu.CompilerParams(
+            collective_id=1, has_side_effects=True, vmem_limit_bytes=48 * 1024 * 1024
+        ),
+    )(
+        feat,
+        cot,
+        src,
+        src_t,
+        dst,
+        dst_t,
+        w_reduce,
+        w_spatial,
+        w_expand,
+        w_short,
+        gm,
+        sm,
+        gw,
+        sw,
+        sel,
+        sel_t,
+        ends,
+    )
+    block_out = landed.reshape(1, spaces * capacity, Q, wide)
+    tot3b, tot2b, tot1b = tot[3], tot[4], tot[5]
 
     lanes = mid
 

time: 195 us -> 163 us (0.84)
  local copies, waits for them, and re-layouts: 45.9 us -> 16.3 us
  starting transfers between devices: 16.1 us -> 0 us
  Pallas kernels: 125 us -> 139 us
    unnamed x128 -> x45, local copies, waits for them, and re-layouts: 39.8 us -> 12.1 us
    pallas_call x15 -> x1, Pallas kernels: 100 us -> 114 us  [body(): pl.pallas_call(functools.partial(whole_kernel, (m_in, m_mid, m_wide), spa...]
    all_to_all x2 -> x0, starting transfers between devices: 11 us -> none  [the longest x1 6.62 us: body(): lax.all_to_all(outgoing.reshape(spaces, capacity * Q, wide), 'space', spl...]
    ppermute x2 -> x0, starting transfers between devices: 5.03 us -> none  [passed_along(): return lax.ppermute(shard, 'space', pairs)]
  transfers between devices with their start and end apart: 4 -> 0, of which waited for: 0 -> 0; matrix products, arithmetic and copies ran while one was open for 6% -> 0% of each run, Pallas kernels for 41% -> 0%
where the time goes in v2:
time: 163 us; the launch traced here: 162 us
  Pallas kernels  139 us (85%)
  local copies, waits for them, and re-layouts  16.3 us (10%)
  other arithmetic  5.45 us (3%)
    pallas_call x1, Pallas kernels, body(): pl.pallas_call(functools.partial(whole_kernel, (m_in, m_mid, m_wide), spa...  114 us
    pallas_call x1, Pallas kernels, share_total(): pl.pallas_call(functools.partial(share_kernel, groups, peers), out_shape=...  25.2 us
    unnamed x45, local copies, waits for them, and re-layouts  12.1 us

profile of v2, /device:TPU:0, one launch (start us, length us, event | category | flops | bytes accessed | tf_op | source)
XLA Modules:
  0.0 161.9 jit_solution(1925744587723917044)
XLA Ops:
  0.6 0.0 copy-start
  0.7 0.0 copy-start.13
  0.7 0.0 copy-start.12
  0.7 0.0 copy-start.15
  0.7 0.0 copy-start.14
  0.7 0.0 copy-start.1
  0.7 1.0 convert_reduce_fusion
  1.7 0.7 fusion.14
  2.4 0.1 pad.10.clone
  2.4 0.7 copy.53
  3.2 0.1 broadcast_in_dim.166
  3.3 0.1 broadcast_in_dim.158
  3.4 0.1 broadcast_in_dim.159
  3.5 0.1 select_select_fusion.3
  3.6 0.1 iota_add_fusion.1
  3.7 0.1 add.553.refs_5_
  3.8 0.1 broadcast_in_dim.164
  3.9 0.1 select_select_fusion.2
  4.0 0.1 broadcast_in_dim.169
  4.1 0.1 broadcast_in_dim.170
  4.2 0.1 broadcast_in_dim.171
  4.3 0.1 broadcast_in_dim.172
  4.4 0.1 iota_add_fusion
  4.6 0.1 add.499
  4.7 0.1 add_add_fusion
  4.8 0.1 sub.99
  4.9 0.1 broadcast_in_dim.177
  5.1 0.1 copy.36.refs_2_
  5.2 0.2 add.556.refs_4_
  5.4 0.0 copy-done
  5.4 0.0 copy-done.13
  5.4 0.0 copy-done.12
  5.5 0.0 copy-start.3
  5.5 1.0 copy-done.3
  6.4 0.9 copy-done.4
  7.4 0.9 copy-done.5
  8.3 0.9 copy-done.6
  9.2 0.9 copy-done.7
  10.1 0.9 copy-done.8
  11.0 113.9 %shard_map.231 = (bf16[2048,512]{1,0:T(8,128)(2,1)}, bf16[8,128,512]{2,1,0:T(8,128)(2,1)S(1)}, bf16[512,128]{1,0:T(8,128)(2,1)S(1)}, bf16[1152,128]{1,0:T(8,128)...) custom-call(bf16[2048,512]{1,0:T(8,128)(2,1)} %bitcast.71, ...), custom_call_target="tpu_custom_call" | custom-call | tf_op jit(solution)/shard_map/pallas_call | solution.py:787
  124.9 0.0 copy-start.2
  124.9 0.8 copy-done.2
  125.7 0.7 copy-done.9
  126.4 0.7 copy-done.11
  127.1 0.1 maximum_maximum_fusion.vec
  127.1 0.9 reshape.890
  128.1 0.0 copy-start.10
  128.1 1.2 reshape.892
  129.3 0.1 copy.39
  129.5 0.1 constant_dynamic-update-slice_fusion
  129.7 0.1 copy.50
  129.7 0.0 copy-start.17
  129.7 25.2 %shard_map.232 = (f32[4,144,128]{2,1,0:T(8,128)S(1)}, f32[8,512]{1,0:T(8,128)S(1)}) custom-call(bf16[4,8,144,128]{3,2,1,0:T(8,128)(2,1)S(1)} %bitcast.63, f32[8,512]{1,0:T(8,128)S(1)} %maximum_maximum_fusion.vec), custom_call_target="tpu_custom_call" | custom-call | tf_op jit(solution)/shard_map/pallas_call | solution.py:622
  155.0 0.6 fusion.5
  155.6 0.6 fusion.3
  156.3 0.6 fusion.2
  157.0 0.6 slice_multiply_fusion.2
  157.6 0.6 copy.52
  158.2 0.6 slice_multiply_fusion.1
  158.9 0.1 copy.42
  159.0 0.7 copy.51
  159.6 1.0 copy.60
  160.6 0.0 copy-done.16
  160.6 1.3 copy.61
  (43 shorter events, 0.3 us)
Async XLA Ops:
  0.6 4.8 %copy-start = (bf16[1,64,16,512]{3,2,1,0:T(8,128)(2,1)S(1)}, bf16[1,64,16,512]{3,2,1,0:T(8,128)(2,1)}, u32[]{:S(2)}) copy-start(bf16[1,64,16,512]{3,2,1,0:T(8,128)(2,1)} %param.27) | copy-start | bytes 3145732
  0.7 4.8 %copy-start.13 = (f32[2,512]{1,0:T(2,128)S(1)}, f32[2,512]{1,0:T(2,128)}, u32[]{:S(2)}) copy-start(f32[2,512]{1,0:T(2,128)} %refs_13_.1) | copy-start | bytes 12292
  0.7 4.8 %copy-start.12 = (f32[2,512]{1,0:T(2,128)S(1)}, f32[2,512]{1,0:T(2,128)}, u32[]{:S(2)}) copy-start(f32[2,512]{1,0:T(2,128)} %refs_12_.1) | copy-start | bytes 12292
  0.7 4.8 %copy-start.15 = (f32[2,128]{1,0:T(2,128)S(1)}, f32[2,128]{1,0:T(2,128)}, u32[]{:S(2)}) copy-start(f32[2,128]{1,0:T(2,128)} %refs_11_.1) | copy-start | bytes 3076
  0.7 4.8 %copy-start.14 = (f32[2,128]{1,0:T(2,128)S(1)}, f32[2,128]{1,0:T(2,128)}, u32[]{:S(2)}) copy-start(f32[2,128]{1,0:T(2,128)} %refs_10_.1) | copy-start | bytes 3076
  0.7 4.8 %copy-start.1 = (bf16[512,512]{1,0:T(8,128)(2,1)S(1)}, bf16[512,512]{1,0:T(8,128)(2,1)}, u32[]{:S(2)}) copy-start(bf16[512,512]{1,0:T(8,128)(2,1)} %refs_9_.1) | copy-start | bytes 1572868
  5.5 1.0 copy-start.3
  6.4 0.9 copy-start.4
  7.4 0.9 copy-start.5
  8.3 0.9 copy-start.6
  9.2 0.9 copy-start.7
  10.1 0.9 copy-start.8
  124.9 0.8 copy-start.2
  125.7 0.7 copy-start.9
  126.4 0.7 copy-start.11
  128.1 1.4 copy-start.10
  129.7 26.6 %copy-start.17 = (f32[2]{0:T(128)S(1)}, f32[2]{0:T(128)}, u32[]{:S(2)}) copy-start(f32[2]{0:T(128)} %constant.81) | copy-start | bytes 28
  159.0 1.6 %copy-start.16 = (bf16[2048,512]{1,0:T(8,128)(2,1)S(1)}, bf16[2048,512]{1,0:T(8,128)(2,1)}, u32[]{:S(2)}) copy-start(bf16[2048,512]{1,0:T(8,128)(2,1)} %get-tuple-element.20) | copy-start | bytes 6291460

commit v3 on v2

--- a/solution.py
+++ b/solution.py
@@ -411,14 +411,20 @@
 
 def whole_kernel(members, peers, *refs):
     m_in, m_mid, m_wide = members
-    (feat, cot, src, src_t, dst, dst_t, w_reduce, w_spatial, w_expand, w_short, gm, sm, gw, sw) = refs[:14]
+    (feat_in, cot, src, src_t, dst, dst_t, w_reduce, w_spatial, w_expand, w_short, gm, sm, gw, sw) = refs[:14]
     sel, sel_t, ends = refs[14:17]
     g_feat, landed, g_reduce, g_spatial, g_expand, g_short, tot = refs[17:24]
     (conv1, sub_in, conv_short, act, rim, prior, columns, conv2, act2, conv3) = refs[24:34]
     (up, outgoing, res, dshort, back2, d3, d2, planes, rim_b, following, back1) = refs[34:45]
-    total, home, moms, slots = refs[45:49]
-    sum_send, sum_recv, cot_send, cot_recv, out_send, out_recv, rim_send, rim_recv = refs[49:]
+    total, home, moms, slots, feat = refs[45:50]
+    sum_send, sum_recv, cot_send, cot_recv, out_send, out_recv, rim_send, rim_recv, own_sem = refs[50:]
     me = lax.axis_index("space")
+    rows = cot.shape[1]
+    mid = conv2.shape[1]
+    feat_copy = pltpu.make_async_copy(feat_in, feat, own_sem.at[0])
+    feat_copy.start()
+    cot_copy = pltpu.make_async_copy(cot.at[me], home.at[:rows], own_sem.at[1])
+    cot_copy.start()
     barrier = pltpu.get_barrier_semaphore()
     for k in range(1, peers):
         pl.semaphore_signal(
@@ -438,44 +444,66 @@
         copy.start()
         return copy
 
-    def slide_total(n):
+    def slide_total(n, width):
         copies = [
-            send(k, moms.at[n], slots.at[n, k], sum_send.at[n, k], sum_recv.at[n, k])
+            send(
+                k,
+                moms.at[n, :, :width],
+                slots.at[n, k, :, :width],
+                sum_send.at[n, k],
+                sum_recv.at[n, k],
+            )
             for k in range(1, peers)
         ]
-        slots[n, 0] = moms[n]
+        slots[n, 0, :, :width] = moms[n, :, :width]
         for copy in copies:
             copy.wait()
-        sum_of = slots[n, me]
+        sum_of = slots[n, me, :, :width]
         for s in range(1, peers):
-            sum_of = sum_of + slots[n, lax.rem(me - s + peers, peers)]
-        tot[n] = sum_of
-
-    rows = cot.shape[1]
-    cot_copies = [
-        send(k, cot.at[lax.rem(me + k, peers)], home.at[block(k, rows)], cot_send.at[k], cot_recv.at[k])
-        for k in range(1, peers)
-    ]
+            sum_of = sum_of + slots[n, lax.rem(me - s + peers, peers), :, :width]
+        tot[n, :, :width] = sum_of
+
+    cot_copies, out_copies = [], []
+
+    def send_cot(first, last):
+        for k in range(1 + (peers - 1) * first // 7, 1 + (peers - 1) * last // 7):
+            to = lax.rem(me + k, peers)
+            cot_copies.append(
+                send(k, cot.at[to], home.at[block(k, rows)], cot_send.at[k], cot_recv.at[k])
+            )
+
+    def send_out(first, last):
+        for k in range(1 + (peers - 1) * first // 7, 1 + (peers - 1) * last // 7):
+            out_copies.append(
+                send(k, outgoing.at[block(k, rows)], landed.at[me], out_send.at[k], out_recv.at[k])
+            )
+
+    wide = conv3.shape[1]
+    tot[...] = jnp.zeros_like(tot)
+    send_cot(0, 2)
+    feat_copy.wait()
     first_kernel(feat, w_reduce, w_short, sel, conv1, sub_in, conv_short, moms.at[0])
-    slide_total(0)
+    slide_total(0, mid)
+    send_cot(2, 3)
     act_kernel(m_in, conv1, tot.at[0], gm, sm, ends, act, rim)
     send(1, rim, prior, rim_send.at[0], rim_recv.at[0]).wait()
+    send_cot(3, 4)
     conv2_kernel(act, prior, src, w_spatial, columns, conv2, moms.at[1])
-    slide_total(1)
+    slide_total(1, mid)
+    send_cot(4, 5)
     conv3_kernel(m_mid, conv2, tot.at[1], gm, sm, w_expand, act2, conv3, moms.at[2])
-    slide_total(2)
-    home[:rows, :] = cot[me]
+    moms[2, 2:4, :] = moms[0, 2:4, :]
+    send_cot(5, 7)
+    slide_total(2, wide)
+    cot_copy.wait()
     for copy in cot_copies:
         copy.wait()
     result_kernel(
-        m_wide, conv3, conv_short, tot.at[2], tot.at[0], gw, sw, dst, dst_t, home, up, outgoing, moms.at[3], res
-    )
-    out_copies = [
-        send(k, outgoing.at[block(k, rows)], landed.at[me], out_send.at[k], out_recv.at[k])
-        for k in range(1, peers)
-    ]
+        m_wide, conv3, conv_short, tot.at[2], tot.at[2], gw, sw, dst, dst_t, home, up, outgoing, moms.at[3], res
+    )
     landed[me] = outgoing[:rows, :]
-    slide_total(3)
+    slide_total(3, wide)
+    send_out(0, 1)
     back3_kernel(
         m_wide,
         m_mid,
@@ -483,7 +511,7 @@
         conv3,
         conv_short,
         tot.at[2],
-        tot.at[0],
+        tot.at[2],
         tot.at[3],
         gw,
         act2,
@@ -500,7 +528,8 @@
         moms.at[4],
         d3,
     )
-    slide_total(4)
+    slide_total(4, mid)
+    send_out(1, 2)
     back2_kernel(
         m_mid,
         back2,
@@ -519,7 +548,8 @@
     )
     send(peers - 1, rim_b, following, rim_send.at[1], rim_recv.at[1]).wait()
     back1_kernel(m_in, planes, following, ends, conv1, tot.at[0], gm, sm, back1, moms.at[5])
-    slide_total(5)
+    slide_total(5, mid)
+    send_out(2, 7)
     last_kernel(
         m_in,
         back1,
@@ -781,13 +811,14 @@
         ((slots, wide), BF16),
         ((6, 8, wide), F32),
         ((6, spaces, 8, wide), F32),
+        (feat.shape, BF16),
     ]
     dma = pltpu.SemaphoreType.DMA
-    semaphores = [dma((6, spaces))] * 2 + [dma((spaces,))] * 4 + [dma((2,))] * 2
+    semaphores = [dma((6, spaces))] * 2 + [dma((spaces,))] * 4 + [dma((2,))] * 3
     g_feat, landed, g_reduce, g_spatial, g_expand, g_short, tot = pl.pallas_call(
         functools.partial(whole_kernel, (m_in, m_mid, m_wide), spaces),
         out_shape=[jax.ShapeDtypeStruct(a, t) for a, t in outs],
-        in_specs=[vmem] * 17,
+        in_specs=[pl.BlockSpec(memory_space=pl.ANY)] * 2 + [vmem] * 15,
         out_specs=[vmem] * len(outs),
         scratch_shapes=[pltpu.VMEM(a, t) for a, t in scratch] + semaphores,
         compiler_params=pltpu.CompilerParams(

time: 163 us -> 146 us (0.90)
  Pallas kernels: 139 us -> 121 us
    pallas_call x1, Pallas kernels: 114 us -> 89.5 us  [body(): pl.pallas_call(functools.partial(whole_kernel, (m_in, m_mid, m_wide), spa...]
    pallas_call x1, Pallas kernels: 25.2 us -> 31.9 us  [share_total(): pl.pallas_call(functools.partial(share_kernel, groups, peers), out_shape=...]
where the time goes in v3:
time: 146 us; the launch traced here: 144 us
  Pallas kernels  121 us (83%)
  local copies, waits for them, and re-layouts  16.3 us (11%)
  other arithmetic  5.45 us (4%)
    pallas_call x1, Pallas kernels, body(): pl.pallas_call(functools.partial(whole_kernel, (m_in, m_mid, m_wide), spa...  89.5 us
    pallas_call x1, Pallas kernels, share_total(): pl.pallas_call(functools.partial(share_kernel, groups, peers), out_shape=...  31.9 us
    unnamed x45, local copies, waits for them, and re-layouts  12.1 us

profile of v3, /device:TPU:0, one launch (start us, length us, event | category | flops | bytes accessed | tf_op | source)
XLA Modules:
  0.0 144.2 jit_solution(3071579279253473306)
XLA Ops:
  0.6 0.0 copy-start
  0.7 0.0 copy-start.13
  0.7 0.0 copy-start.12
  0.7 0.0 copy-start.15
  0.7 0.0 copy-start.14
  0.7 0.0 copy-start.1
  0.7 1.0 convert_reduce_fusion
  1.7 0.7 fusion.14
  2.4 0.1 pad.10.clone
  2.4 0.7 copy.53
  3.2 0.1 broadcast_in_dim.166
  3.3 0.1 broadcast_in_dim.158
  3.4 0.1 broadcast_in_dim.159
  3.5 0.1 select_select_fusion.3
  3.6 0.1 iota_add_fusion.1
  3.7 0.1 add.553.refs_5_
  3.8 0.1 broadcast_in_dim.164
  3.9 0.1 select_select_fusion.2
  4.0 0.1 broadcast_in_dim.169
  4.1 0.1 broadcast_in_dim.170
  4.2 0.1 broadcast_in_dim.171
  4.3 0.1 broadcast_in_dim.172
  4.4 0.1 iota_add_fusion
  4.6 0.1 add.499
  4.7 0.1 add_add_fusion
  4.8 0.1 sub.99
  4.9 0.1 broadcast_in_dim.177
  5.1 0.1 copy.36.refs_2_
  5.2 0.2 add.556.refs_4_
  5.4 0.0 copy-done
  5.4 0.0 copy-done.13
  5.4 0.0 copy-done.12
  5.5 0.0 copy-start.3
  5.5 1.0 copy-done.3
  6.4 0.9 copy-done.4
  7.4 0.9 copy-done.5
  8.3 0.9 copy-done.6
  9.2 0.9 copy-done.7
  10.1 0.9 copy-done.8
  11.0 89.5 %shard_map.231 = (bf16[2048,512]{1,0:T(8,128)(2,1)}, bf16[8,128,512]{2,1,0:T(8,128)(2,1)S(1)}, bf16[512,128]{1,0:T(8,128)(2,1)S(1)}, bf16[1152,128]{1,0:T(8,128)...) custom-call(bf16[2048,512]{1,0:T(8,128)(2,1)} %bitcast.71, ...), custom_call_target="tpu_custom_call" | custom-call | tf_op jit(solution)/shard_map/pallas_call | solution.py:818
  100.5 0.0 copy-start.2
  100.5 0.8 copy-done.2
  101.3 0.7 copy-done.9
  101.9 0.7 copy-done.11
  102.6 0.1 maximum_maximum_fusion.vec
  102.7 0.9 reshape.890
  103.6 0.0 copy-start.10
  103.7 1.2 reshape.892
  104.9 0.1 copy.39
  105.1 0.1 constant_dynamic-update-slice_fusion
  105.2 0.1 copy.50
  105.3 0.0 copy-start.17
  105.3 31.9 %shard_map.232 = (f32[4,144,128]{2,1,0:T(8,128)S(1)}, f32[8,512]{1,0:T(8,128)S(1)}) custom-call(bf16[4,8,144,128]{3,2,1,0:T(8,128)(2,1)S(1)} %bitcast.63, f32[8,512]{1,0:T(8,128)S(1)} %maximum_maximum_fusion.vec), custom_call_target="tpu_custom_call" | custom-call | tf_op jit(solution)/shard_map/pallas_call | solution.py:652
  137.3 0.6 fusion.5
  137.9 0.6 fusion.3
  138.6 0.0 copy-done.17
  138.6 0.6 fusion.2
  139.2 0.6 slice_multiply_fusion.2
  139.9 0.6 copy.52
  140.5 0.6 slice_multiply_fusion.1
  141.1 0.1 copy.42
  141.2 0.7 copy.51
  141.9 1.0 copy.60
  142.9 1.3 copy.61
  (43 shorter events, 0.3 us)
Async XLA Ops:
  0.6 4.8 %copy-start = (bf16[1,64,16,512]{3,2,1,0:T(8,128)(2,1)S(1)}, bf16[1,64,16,512]{3,2,1,0:T(8,128)(2,1)}, u32[]{:S(2)}) copy-start(bf16[1,64,16,512]{3,2,1,0:T(8,128)(2,1)} %param.27) | copy-start | bytes 3145732
  0.7 4.8 %copy-start.13 = (f32[2,512]{1,0:T(2,128)S(1)}, f32[2,512]{1,0:T(2,128)}, u32[]{:S(2)}) copy-start(f32[2,512]{1,0:T(2,128)} %refs_13_.1) | copy-start | bytes 12292
  0.7 4.8 %copy-start.12 = (f32[2,512]{1,0:T(2,128)S(1)}, f32[2,512]{1,0:T(2,128)}, u32[]{:S(2)}) copy-start(f32[2,512]{1,0:T(2,128)} %refs_12_.1) | copy-start | bytes 12292
  0.7 4.8 %copy-start.15 = (f32[2,128]{1,0:T(2,128)S(1)}, f32[2,128]{1,0:T(2,128)}, u32[]{:S(2)}) copy-start(f32[2,128]{1,0:T(2,128)} %refs_11_.1) | copy-start | bytes 3076
  0.7 4.8 %copy-start.14 = (f32[2,128]{1,0:T(2,128)S(1)}, f32[2,128]{1,0:T(2,128)}, u32[]{:S(2)}) copy-start(f32[2,128]{1,0:T(2,128)} %refs_10_.1) | copy-start | bytes 3076
  0.7 4.8 %copy-start.1 = (bf16[512,512]{1,0:T(8,128)(2,1)S(1)}, bf16[512,512]{1,0:T(8,128)(2,1)}, u32[]{:S(2)}) copy-start(bf16[512,512]{1,0:T(8,128)(2,1)} %refs_9_.1) | copy-start | bytes 1572868
  5.5 1.0 copy-start.3
  6.4 0.9 copy-start.4
  7.4 0.9 copy-start.5
  8.3 0.9 copy-start.6
  9.2 0.9 copy-start.7
  10.1 0.9 copy-start.8
  100.5 0.8 copy-start.2
  101.3 0.7 copy-start.9
  101.9 0.7 copy-start.11
  103.6 1.4 copy-start.10
  105.3 33.3 %copy-start.17 = (f32[2]{0:T(128)S(1)}, f32[2]{0:T(128)}, u32[]{:S(2)}) copy-start(f32[2]{0:T(128)} %constant.81) | copy-start | bytes 28
  141.2 1.6 %copy-start.16 = (bf16[2048,512]{1,0:T(8,128)(2,1)S(1)}, bf16[2048,512]{1,0:T(8,128)(2,1)}, u32[]{:S(2)}) copy-start(bf16[2048,512]{1,0:T(8,128)(2,1)} %get-tuple-element.20) | copy-start | bytes 6291460
